TPU v7x, 32 devices: a whole 2x2x4 slice. The times are simulated.
32 devices in a mesh: dp: 4 (over y, x), expert: 8 (over z, core).
Axes of the slice: x: 2, y: 2, z: 4, core: 2. Of those that a mesh axis runs over, the one named last changes fastest.
Arguments:
- tokens: bfloat16 [4096, 2048], P(('dp', 'expert')), may hold values from -6 to 6
- expert_ids: int32 [4096, 1], P(('dp', 'expert')), may hold values from 0 to 7; in each aligned block of 128 rows (0 to 127, 128 to 255, ...) at most 20 rows name the same one
- route_weight: float32 [4096, 1], P(('dp', 'expert')), may hold values from 0.1 to 1
- cotangent: bfloat16 [4096, 2048], P(('dp', 'expert')), may hold values from -0.59765625 to 0.59765625
- w_gate: bfloat16 [8192, 2048], P('expert', 'dp'), may hold values from -0.125 to 0.125
- w_up: bfloat16 [8192, 2048], P('expert', 'dp'), may hold values from -0.125 to 0.125
- w_down: bfloat16 [8192, 2048], P('expert', 'dp'), may hold values from -0.1875 to 0.1875
Outputs:
- layer_out: bfloat16 [4096, 2048], P(('dp', 'expert'))
- token_grad: bfloat16 [4096, 2048], P(('dp', 'expert'))
- gate_grad: bfloat16 [8192, 2048], P('expert', 'dp')
- up_grad: bfloat16 [8192, 2048], P('expert', 'dp')
- down_grad: bfloat16 [8192, 2048], P('expert', 'dp')
Inputs may be any that keep to these rules, and one draw needn't show every extreme that they name: `expert_ids`: among the 128 rows of one device, at most 20 name the same expert.
All inputs are finite; a program needn't handle non-finite values.
Results may differ from a plain program's by a relative error of at most 0.018.
Values may be sent and summed in bfloat16 or wider, within the bound.
A program may use at most 64 MiB of HBM per device.

v0:
```python
import jax
import jax.numpy as jnp
from jax import lax
from jax.sharding import PartitionSpec as P

EXPERTS = 8
CAP = 20


def spread_rows(blocks, group_size):
    features = blocks.shape[2]
    sending = jnp.repeat(blocks, group_size, axis=0)
    arrived = lax.all_to_all(sending, "expert", split_axis=0, concat_axis=0, tiled=True)
    result = arrived.reshape(-1, features)
    return result


def gather_back(partial_value, group_size):
    features = partial_value.shape[1]
    sending = partial_value.astype(jnp.bfloat16).reshape(lax.axis_size("expert"), -1, features)
    arrived = lax.all_to_all(sending, "expert", split_axis=0, concat_axis=0, tiled=True)
    summed = jnp.sum(arrived.reshape(EXPERTS, group_size, -1, features).astype(jnp.float32), axis=1)
    result = summed.reshape(-1, features)
    return result


def local(tokens, expert_ids, route_weight, cotangent, w_gate, w_up, w_down):
    features = tokens.shape[1]
    group_size = lax.axis_size("expert") // EXPERTS
    chosen = expert_ids[:, 0]
    onehot = (chosen[:, None] == jnp.arange(EXPERTS, dtype=jnp.int32)[None, :]).astype(jnp.int32)
    before = jnp.cumsum(onehot, axis=0) - onehot
    slot_index = chosen * CAP + jnp.sum(before * onehot, axis=1)
    placing = (jnp.arange(EXPERTS * CAP, dtype=jnp.int32)[:, None] == slot_index[None, :]).astype(
        jnp.bfloat16
    )
    scaled = (route_weight * cotangent.astype(jnp.float32)).astype(jnp.bfloat16)
    token_slots = (
        jnp.dot(placing, tokens, preferred_element_type=jnp.float32)
        .astype(jnp.bfloat16)
        .reshape(EXPERTS, CAP, features)
    )
    grad_slots = (
        jnp.dot(placing, scaled, preferred_element_type=jnp.float32)
        .astype(jnp.bfloat16)
        .reshape(EXPERTS, CAP, features)
    )
    gate_full, up_full, down_full = (
        lax.all_gather(w_gate, "dp", axis=1, tiled=True),
        lax.all_gather(w_up, "dp", axis=1, tiled=True),
        lax.all_gather(w_down, "dp", axis=1, tiled=True),
    )
    token_rows = spread_rows(token_slots, group_size)
    gate_pre = jnp.einsum("nd,hd->nh", token_rows, gate_full, preferred_element_type=jnp.float32)
    up_pre = jnp.einsum("nd,hd->nh", token_rows, up_full, preferred_element_type=jnp.float32)
    gate_sigmoid = jax.nn.sigmoid(gate_pre)
    gate_silu = gate_pre * gate_sigmoid
    hidden = (gate_silu * up_pre).astype(jnp.bfloat16)
    out_slots = gather_back(
        jnp.dot(hidden, down_full, preferred_element_type=jnp.float32), group_size
    )
    layer_out = (route_weight * jnp.take(out_slots, slot_index, axis=0)).astype(jnp.bfloat16)
    grad_rows = spread_rows(grad_slots, group_size)
    hidden_grad = jnp.einsum("nd,hd->nh", grad_rows, down_full, preferred_element_type=jnp.float32)
    gate_grad_pre = (
        hidden_grad * up_pre * (gate_sigmoid * (1.0 + gate_pre * (1.0 - gate_sigmoid)))
    ).astype(jnp.bfloat16)
    up_grad_pre = (hidden_grad * gate_silu).astype(jnp.bfloat16)
    input_term = jnp.dot(gate_grad_pre, gate_full, preferred_element_type=jnp.float32) + jnp.dot(
        up_grad_pre, up_full, preferred_element_type=jnp.float32
    )
    back_slots = gather_back(input_term, group_size)
    token_grad = jnp.take(back_slots, slot_index, axis=0).astype(jnp.bfloat16)
    gate_term = jnp.einsum(
        "nh,nd->hd", gate_grad_pre, token_rows, preferred_element_type=jnp.float32
    )
    up_term = jnp.einsum("nh,nd->hd", up_grad_pre, token_rows, preferred_element_type=jnp.float32)
    down_term = jnp.einsum("nh,nd->hd", hidden, grad_rows, preferred_element_type=jnp.float32)
    gate_grad, up_grad, down_grad = (
        lax.psum_scatter(
            gate_term.astype(jnp.bfloat16), "dp", scatter_dimension=1, tiled=True
        ).astype(jnp.float32),
        lax.psum_scatter(
            up_term.astype(jnp.bfloat16), "dp", scatter_dimension=1, tiled=True
        ).astype(jnp.float32),
        lax.psum_scatter(
            down_term.astype(jnp.bfloat16), "dp", scatter_dimension=1, tiled=True
        ).astype(jnp.float32),
    )
    return (
        layer_out,
        token_grad,
        gate_grad.astype(jnp.bfloat16),
        up_grad.astype(jnp.bfloat16),
        down_grad.astype(jnp.bfloat16),
    )


def solution(mesh):
    return jax.shard_map(
        local,
        mesh=mesh,
        in_specs=(
            P(("dp", "expert"), None),
            P(("dp", "expert"), None),
            P(("dp", "expert"), None),
            P(("dp", "expert"), None),
            P("expert", "dp"),
            P("expert", "dp"),
            P("expert", "dp"),
        ),
        out_specs=(
            P(("dp", "expert"), None),
            P(("dp", "expert"), None),
            P("expert", "dp"),
            P("expert", "dp"),
            P("expert", "dp"),
        ),
        check_vma=False,
    )
```

profile of v0, /device:TPU:0, one launch (start us, length us, event | category | flops | bytes accessed | tf_op | source)
XLA Modules:
  0.0 353.6 jit_solution(16938884996230069525)
XLA Ops:
  7.2 0.7 all-gather.4.cloned.1.call-update
  7.9 0.0 all-gather.6.cloned.1.call-start
  8.0 0.7 all-gather.6.cloned.1.call-update
  8.7 0.7 all-gather.8.cloned.1.call-update
  9.4 0.7 fusion.4
  10.2 0.2 reduce_window_sum.11
  10.3 0.8 select_reduce_fusion
  11.2 0.7 compare_and_fusion
  11.8 0.3 convolution_convert_fusion.5
  12.2 1.0 reshape_broadcast_in_dim_reshape.6
  13.2 6.3 %all-to-all-start = ((bf16[8,20,2048]{2,1,0:T(8,128)(2,1)}), bf16[8,20,2048]{2,1,0:T(8,128)(2,1)S(1)}, u32[]{:S(2)}, u32[]{:S(2)}) async-start(bf16[8,20,2048]{2,1,0:T(8,128)(2,1)} %reshape_broadcast_in_dim_reshape.6), calls=%async_computation | async-start | bytes 1572864 | tf_op jit(solution)/shard_map/all_to_all | solution.py:13
  19.5 0.4 convolution_convert_fusion.3
  19.9 1.0 reshape_broadcast_in_dim_reshape.7
  21.0 19.5 %all-to-all-done = bf16[8,20,2048]{2,1,0:T(8,128)(2,1)S(1)} async-done(((bf16[8,20,2048]{2,1,0:T(8,128)(2,1)}), bf16[8,20,2048]{2,1,0:T(8,128)(2,1)S(1)}, u32[]{:S(2)}, u32[]{:S(2)}) %all-to-all-start) | async-done | bytes 655392 | tf_op jit(solution)/shard_map/all_to_all | solution.py:13
  40.5 3.6 %all-to-all-start.2 = ((bf16[8,20,2048]{2,1,0:T(8,128)(2,1)}), bf16[8,20,2048]{2,1,0:T(8,128)(2,1)S(1)}, u32[]{:S(2)}, u32[]{:S(2)}) async-start(bf16[8,20,2048]{2,1,0:T(8,128)(2,1)} %reshape_broadcast_in_dim_reshape.7), calls=%async_computation.2 | async-start | bytes 1572864 | tf_op jit(solution)/shard_map/all_to_all | solution.py:13
  44.1 0.0 reduce-scatter.4.cloned.1.call-start
  44.1 0.1 reshape.57
  44.2 20.7 %all-to-all-done.2 = bf16[8,20,2048]{2,1,0:T(8,128)(2,1)S(1)} async-done(((bf16[8,20,2048]{2,1,0:T(8,128)(2,1)}), bf16[8,20,2048]{2,1,0:T(8,128)(2,1)S(1)}, u32[]{:S(2)}, u32[]{:S(2)}) %all-to-all-start.2) | async-done | bytes 655392 | tf_op jit(solution)/shard_map/all_to_all | solution.py:13
  64.9 0.1 reshape.61
  65.1 0.1 all-gather.4.cloned.1.call-done
  65.2 4.6 %fusion.7 = f32[160,1024]{1,0:T(8,128)} fusion(bf16[160,2048]{1,0:T(8,128)(2,1)S(1)} %reshape.57, bf16[1024,2048]{1,0:T(8,128)(2,1)} %all-gather.4.cloned.1.call-done), kind=kOutput, calls=%fused_computation.30 | convolution fusion | flops 671088640 | bytes 5505024 | tf_op jit(solution)/shard_map/nd,hd->nh/dot_general | solution.py:54
  69.7 49.9 %all-gather.6.cloned.1.call-done = bf16[1024,2048]{1,0:T(8,128)(2,1)} async-done(((bf16[1024,512]{1,0:T(8,128)(2,1)}), bf16[1024,2048]{1,0:T(8,128)(2,1)}) %all-gather.6.cloned.1.call-update) | async-done | bytes 4194320 | tf_op jit(solution)/shard_map/all_gather | solution.py:50
  119.6 4.6 %fusion.8 = f32[160,1024]{1,0:T(8,128)} fusion(bf16[160,2048]{1,0:T(8,128)(2,1)S(1)} %reshape.57, bf16[1024,2048]{1,0:T(8,128)(2,1)} %all-gather.6.cloned.1.call-done), kind=kOutput, calls=%fused_computation.31 | convolution fusion | flops 671088640 | bytes 5505024 | tf_op jit(solution)/shard_map/nd,hd->nh/dot_general | solution.py:55
  124.1 49.9 %all-gather.8.cloned.1.call-done = bf16[1024,2048]{1,0:T(8,128)(2,1)} async-done(((bf16[1024,512]{1,0:T(8,128)(2,1)}), bf16[1024,2048]{1,0:T(8,128)(2,1)}) %all-gather.8.cloned.1.call-update) | async-done | bytes 4194320 | tf_op jit(solution)/shard_map/all_gather | solution.py:51
  174.0 4.2 %multiply_convert_fusion.1 = (bf16[160,1024]{1,0:T(8,128)(2,1)S(1)}, bf16[160,1024]{1,0:T(8,128)(2,1)S(1)}, bf16[160,1024]{1,0:T(8,128)(2,1)S(1)}) fusion(f32[160,1024]{1,0:T(8,128)} %fusion.7, f32[160,1024]{1,0:T(8,128)} %fusion.8, bf16[160,2048]{1,0:T(8,128)(2,1)S(1)} %reshape.61, bf16[1024,2048]{1,0:T(8,128)(2,1)} %all-gather.8.cloned.1.call-done), kind=kOutput, calls=%fused_computation.14 | convolution fusion | flops 673546240 | bytes 7143424 | tf_op jit(solution)/shard_map/nd,hd->nh/dot_general | solution.py:64
  178.2 3.3 convolution_convert_fusion.2
  181.5 0.0 reduce-scatter.6.cloned.1.call-start
  181.6 3.3 convolution_convert_fusion.1
  184.9 0.0 reduce-scatter.8.cloned.1.call-start
  184.9 3.3 convolution_convert_fusion
  188.2 3.2 fusion.9
  191.5 0.3 copy-done.1
  191.8 0.9 fusion
  192.7 1.0 reshape.62
  193.7 4.8 %all-to-all-start.3 = ((bf16[8,20,2048]{2,1,0:T(8,128)(2,1)}), bf16[8,20,2048]{2,1,0:T(8,128)(2,1)S(1)}, u32[]{:S(2)}, u32[]{:S(2)}) async-start(bf16[8,20,2048]{2,1,0:T(8,128)(2,1)} %reshape.62), calls=%async_computation.3 | async-start | bytes 1572864 | tf_op jit(solution)/shard_map/all_to_all | solution.py:21
  198.5 3.1 convolution_convert_fusion.4
  201.6 1.1 reshape.58
  202.7 16.8 %all-to-all-done.3 = bf16[8,20,2048]{2,1,0:T(8,128)(2,1)S(1)} async-done(((bf16[8,20,2048]{2,1,0:T(8,128)(2,1)}), bf16[8,20,2048]{2,1,0:T(8,128)(2,1)S(1)}, u32[]{:S(2)}, u32[]{:S(2)}) %all-to-all-start.3) | async-done | bytes 655392 | tf_op jit(solution)/shard_map/all_to_all | solution.py:21
  219.5 3.5 %all-to-all-start.1 = ((bf16[8,20,2048]{2,1,0:T(8,128)(2,1)}), bf16[8,20,2048]{2,1,0:T(8,128)(2,1)S(1)}, u32[]{:S(2)}, u32[]{:S(2)}) async-start(bf16[8,20,2048]{2,1,0:T(8,128)(2,1)} %reshape.58), calls=%async_computation.1 | async-start | bytes 1572864 | tf_op jit(solution)/shard_map/all_to_all | solution.py:21
  223.1 0.1 reshape.68
  223.2 0.9 gather_fusion.1
  224.1 19.8 %all-to-all-done.1 = bf16[8,20,2048]{2,1,0:T(8,128)(2,1)S(1)} async-done(((bf16[8,20,2048]{2,1,0:T(8,128)(2,1)}), bf16[8,20,2048]{2,1,0:T(8,128)(2,1)S(1)}, u32[]{:S(2)}, u32[]{:S(2)}) %all-to-all-start.1) | async-done | bytes 655392 | tf_op jit(solution)/shard_map/all_to_all | solution.py:21
  243.9 0.1 reshape.66
  244.1 1.0 gather_fusion
  245.0 1.0 select_convert_fusion
  246.0 1.0 fusion.1
  247.0 43.7 %reduce-scatter.6.cloned.1.call-done = bf16[1024,512]{1,0:T(8,128)(2,1)} async-done(((bf16[1024,2048]{1,0:T(8,128)(2,1)}), bf16[1024,512]{1,0:T(8,128)(2,1)}) %reduce-scatter.6.cloned.1.call-update) | async-done | bytes 1048592 | tf_op jit(solution)/shard_map/reduce_scatter | solution.py:83
  290.7 56.1 %reduce-scatter.8.cloned.1.call-done = bf16[1024,512]{1,0:T(8,128)(2,1)} async-done(((bf16[1024,2048]{1,0:T(8,128)(2,1)}), bf16[1024,512]{1,0:T(8,128)(2,1)}) %reduce-scatter.8.cloned.1.call-update) | async-done | bytes 1048592 | tf_op jit(solution)/shard_map/reduce_scatter | solution.py:86
  (15 shorter events, 0.2 us)
Async XLA Ops:
  7.2 4.7 %copy-start = (bf16[128,2048]{1,0:T(8,128)(2,1)S(1)}, bf16[128,2048]{1,0:T(8,128)(2,1)}, u32[]{:S(2)}) copy-start(bf16[128,2048]{1,0:T(8,128)(2,1)} %param.9) | copy-start | bytes 1572868
  7.2 12.3 %copy-start.3 = (f32[128,1]{0,1:T(1,128)S(1)}, f32[128,1]{0,1:T(1,128)}, u32[]{:S(2)}) copy-start(f32[128,1]{0,1:T(1,128)} %param.11) | copy-start | bytes 1540
  7.2 12.3 %copy-start.2 = (bf16[128,2048]{1,0:T(8,128)(2,1)S(1)}, bf16[128,2048]{1,0:T(8,128)(2,1)}, u32[]{:S(2)}) copy-start(bf16[128,2048]{1,0:T(8,128)(2,1)} %param.12) | copy-start | bytes 1572868
  7.2 58.0 %all-gather.4.cloned.1.call-start = ((), (), s32[]{:S(2)}) async-start(), calls=%async_computation.7 | async-start | bytes 5242880 | tf_op jit(solution)/shard_map/all_gather | solution.py:49
  7.9 111.7 %all-gather.6.cloned.1.call-start = ((), (), s32[]{:S(2)}) async-start(), calls=%async_computation.8 | async-start | bytes 5242880 | tf_op jit(solution)/shard_map/all_gather | solution.py:50
  8.7 165.3 %all-gather.8.cloned.1.call-start = ((), (), s32[]{:S(2)}) async-start(), calls=%async_computation.9 | async-start | bytes 5242880 | tf_op jit(solution)/shard_map/all_gather | solution.py:51
  13.2 27.3 %all-to-all-start = ((bf16[8,20,2048]{2,1,0:T(8,128)(2,1)}), bf16[8,20,2048]{2,1,0:T(8,128)(2,1)S(1)}, u32[]{:S(2)}, u32[]{:S(2)}) async-start(bf16[8,20,2048]{2,1,0:T(8,128)(2,1)} %reshape_broadcast_in_dim_reshape.6), calls=%async_computation | async-start | bytes 1572864 | tf_op jit(solution)/shard_map/all_to_all | solution.py:13
  40.5 24.5 %all-to-all-start.2 = ((bf16[8,20,2048]{2,1,0:T(8,128)(2,1)}), bf16[8,20,2048]{2,1,0:T(8,128)(2,1)S(1)}, u32[]{:S(2)}, u32[]{:S(2)}) async-start(bf16[8,20,2048]{2,1,0:T(8,128)(2,1)} %reshape_broadcast_in_dim_reshape.7), calls=%async_computation.2 | async-start | bytes 1572864 | tf_op jit(solution)/shard_map/all_to_all | solution.py:13
  44.1 202.9 %reduce-scatter.4.cloned.1.call-start = ((), (), s32[]{:S(2)}) async-start(), calls=%async_computation.10 | async-start | bytes 5242880 | tf_op jit(solution)/shard_map/reduce_scatter | solution.py:80
  181.5 109.1 %reduce-scatter.6.cloned.1.call-start = ((), (), s32[]{:S(2)}) async-start(), calls=%async_computation.11 | async-start | bytes 5242880 | tf_op jit(solution)/shard_map/reduce_scatter | solution.py:83
  184.9 161.9 %reduce-scatter.8.cloned.1.call-start = ((), (), s32[]{:S(2)}) async-start(), calls=%async_computation.12 | async-start | bytes 5242880 | tf_op jit(solution)/shard_map/reduce_scatter | solution.py:86
  188.2 3.6 %copy-start.1 = (bf16[1024,2048]{1,0:T(8,128)(2,1)S(1)}, bf16[1024,2048]{1,0:T(8,128)(2,1)}, u32[]{:S(2)}) copy-start(bf16[1024,2048]{1,0:T(8,128)(2,1)} %all-gather.6.cloned.1.call-done) | copy-start | bytes 12582916
  193.7 25.8 %all-to-all-start.3 = ((bf16[8,20,2048]{2,1,0:T(8,128)(2,1)}), bf16[8,20,2048]{2,1,0:T(8,128)(2,1)S(1)}, u32[]{:S(2)}, u32[]{:S(2)}) async-start(bf16[8,20,2048]{2,1,0:T(8,128)(2,1)} %reshape.62), calls=%async_computation.3 | async-start | bytes 1572864 | tf_op jit(solution)/shard_map/all_to_all | solution.py:21
  219.5 24.5 %all-to-all-start.1 = ((bf16[8,20,2048]{2,1,0:T(8,128)(2,1)}), bf16[8,20,2048]{2,1,0:T(8,128)(2,1)S(1)}, u32[]{:S(2)}, u32[]{:S(2)}) async-start(bf16[8,20,2048]{2,1,0:T(8,128)(2,1)} %reshape.58), calls=%async_computation.1 | async-start | bytes 1572864 | tf_op jit(solution)/shard_map/all_to_all | solution.py:21
Sparse Core Ops, SparseCore 0:
  9.9 55.2 all-gather.3
  67.0 52.5 all-gather.5
  121.4 52.5 all-gather.7
  181.6 52.6 reduce-scatter.3
  238.0 52.6 reduce-scatter.5
  294.1 52.6 reduce-scatter.7
where the time goes:
time: 354 us
  waiting for transfers between devices  278 us (79%)
  matrix products  31.1 us (9%)
  starting transfers between devices  18.5 us (5%)
  between operations  14.3 us (4%)
  local copies, waits for them, and re-layouts  6.9 us (2%)
  other arithmetic  4.34 us (1%)
    reduce_scatter x1, waiting for transfers between devices, local(): lax.psum_scatter(down_term.astype(jnp.bfloat16), 'dp', scatter_dimension=...  56.1 us
    all_gather x1, waiting for transfers between devices, local(): lax.all_gather(w_down, 'dp', axis=1, tiled=True)  49.9 us
    all_gather x1, waiting for transfers between devices, local(): lax.all_gather(w_up, 'dp', axis=1, tiled=True)  49.9 us
    reduce_scatter x1, waiting for transfers between devices, local(): lax.psum_scatter(up_term.astype(jnp.bfloat16), 'dp', scatter_dimension=1,...  43.7 us
    all_to_all x2, waiting for transfers between devices, spread_rows(): lax.all_to_all(sending, 'expert', split_axis=0, concat_axis=0, tiled=True)  40.2 us
    all_to_all x2, waiting for transfers between devices, gather_back(): lax.all_to_all(sending, 'expert', split_axis=0, concat_axis=0, tiled=True)  36.6 us
    all_to_all x2, starting transfers between devices, spread_rows(): lax.all_to_all(sending, 'expert', split_axis=0, concat_axis=0, tiled=True)  9.88 us
    all_to_all x2, starting transfers between devices, gather_back(): lax.all_to_all(sending, 'expert', split_axis=0, concat_axis=0, tiled=True)  8.35 us
  transfers between devices with their start and end apart: 10, of which 9 were waited for; matrix products, arithmetic and copies ran while one was open for 10% of the time, Pallas kernels for 0%

commit v1 on v0

v1 whole, which is shorter than its diff:
```python
import jax
import jax.numpy as jnp
from jax import lax
from jax.sharding import PartitionSpec as P

EXPERTS = 8
CAP = 20
BOTH = ("dp", "expert")


def spread(slots, cols, group_size):
    n_dp = lax.axis_size("dp")
    pieces = slots.reshape(EXPERTS, CAP, n_dp, cols).transpose(2, 0, 1, 3)
    sending = jnp.repeat(pieces, group_size, axis=1).reshape(-1, CAP, cols)
    arrived = lax.all_to_all(sending, BOTH, split_axis=0, concat_axis=0, tiled=True)
    return arrived.reshape(-1, cols)


def bring_back(rows, cols, group_size):
    n_dp = lax.axis_size("dp")
    sending = rows.astype(jnp.bfloat16).reshape(-1, CAP, cols)
    arrived = lax.all_to_all(sending, BOTH, split_axis=0, concat_axis=0, tiled=True)
    pieces = arrived.reshape(n_dp, EXPERTS, group_size, CAP, cols)
    if group_size > 1:
        pieces = jnp.sum(pieces.astype(jnp.float32), axis=2).astype(jnp.bfloat16)
    else:
        pieces = pieces[:, :, 0]
    return pieces.transpose(1, 2, 0, 3).reshape(EXPERTS * CAP, n_dp * cols)


def scatter_sum(partial):
    return lax.psum_scatter(
        partial.astype(jnp.bfloat16), "dp", scatter_dimension=0, tiled=True
    ).astype(jnp.float32)


def local(tokens, expert_ids, route_weight, cotangent, w_gate, w_up, w_down):
    cols = w_gate.shape[1]
    group_size = lax.axis_size("expert") // EXPERTS
    chosen = expert_ids[:, 0]
    onehot = (chosen[:, None] == jnp.arange(EXPERTS, dtype=jnp.int32)[None, :]).astype(jnp.int32)
    before = jnp.cumsum(onehot, axis=0) - onehot
    slot_index = chosen * CAP + jnp.sum(before * onehot, axis=1)
    placing = (jnp.arange(EXPERTS * CAP, dtype=jnp.int32)[:, None] == slot_index[None, :]).astype(
        jnp.bfloat16
    )
    scaled = (route_weight * cotangent.astype(jnp.float32)).astype(jnp.bfloat16)
    token_slots = jnp.dot(placing, tokens, preferred_element_type=jnp.float32).astype(jnp.bfloat16)
    grad_slots = jnp.dot(placing, scaled, preferred_element_type=jnp.float32).astype(jnp.bfloat16)
    token_rows = spread(token_slots, cols, group_size)
    gate_pre = scatter_sum(
        jnp.einsum("nd,hd->nh", token_rows, w_gate, preferred_element_type=jnp.float32)
    )
    up_pre = scatter_sum(
        jnp.einsum("nd,hd->nh", token_rows, w_up, preferred_element_type=jnp.float32)
    )
    grad_rows = spread(grad_slots, cols, group_size)
    hidden_grad = scatter_sum(
        jnp.einsum("nd,hd->nh", grad_rows, w_down, preferred_element_type=jnp.float32)
    )
    gate_sigmoid = jax.nn.sigmoid(gate_pre)
    gate_silu = gate_pre * gate_sigmoid
    hidden = (gate_silu * up_pre).astype(jnp.bfloat16)
    hidden = lax.all_gather(hidden, "dp", axis=0, tiled=True)
    gate_grad_pre = (
        hidden_grad * up_pre * (gate_sigmoid * (1.0 + gate_pre * (1.0 - gate_sigmoid)))
    ).astype(jnp.bfloat16)
    gate_grad_pre = lax.all_gather(gate_grad_pre, "dp", axis=0, tiled=True)
    up_grad_pre = (hidden_grad * gate_silu).astype(jnp.bfloat16)
    up_grad_pre = lax.all_gather(up_grad_pre, "dp", axis=0, tiled=True)
    out_slots = bring_back(
        jnp.dot(hidden, w_down, preferred_element_type=jnp.float32), cols, group_size
    )
    input_term = jnp.dot(gate_grad_pre, w_gate, preferred_element_type=jnp.float32) + jnp.dot(
        up_grad_pre, w_up, preferred_element_type=jnp.float32
    )
    back_slots = bring_back(input_term, cols, group_size)
    picked = jnp.einsum("st,sd->td", placing, out_slots, preferred_element_type=jnp.float32)
    layer_out = (route_weight * picked).astype(jnp.bfloat16)
    token_grad = jnp.einsum(
        "st,sd->td", placing, back_slots, preferred_element_type=jnp.float32
    ).astype(jnp.bfloat16)
    gate_grad = jnp.einsum("nh,nd->hd", gate_grad_pre, token_rows, preferred_element_type=jnp.float32)
    up_grad = jnp.einsum("nh,nd->hd", up_grad_pre, token_rows, preferred_element_type=jnp.float32)
    down_grad = jnp.einsum("nh,nd->hd", hidden, grad_rows, preferred_element_type=jnp.float32)
    return (
        layer_out,
        token_grad,
        gate_grad.astype(jnp.bfloat16),
        up_grad.astype(jnp.bfloat16),
        down_grad.astype(jnp.bfloat16),
    )


def solution(mesh):
    return jax.shard_map(
        local,
        mesh=mesh,
        in_specs=(
            P(BOTH, None),
            P(BOTH, None),
            P(BOTH, None),
            P(BOTH, None),
            P("expert", "dp"),
            P("expert", "dp"),
            P("expert", "dp"),
        ),
        out_specs=(
            P(BOTH, None),
            P(BOTH, None),
            P("expert", "dp"),
            P("expert", "dp"),
            P("expert", "dp"),
        ),
        check_vma=False,
    )
```

time: 354 us -> 279 us (0.79)
  waiting for transfers between devices: 278 us -> 164 us
  blocking collectives: 0 us -> 53.1 us
  starting transfers between devices: 18.5 us -> 8.99 us
  matrix products: 31.1 us -> 27 us
    all_to_all x4 -> x2, waiting for transfers between devices: 76.8 us -> 12.6 us  [bring_back(): lax.all_to_all(sending, BOTH, split_axis=0, concat_axis=0, tiled=True)]
    all_to_all x0 -> x2, blocking collectives: none -> 53.1 us  [spread(): lax.all_to_all(sending, BOTH, split_axis=0, concat_axis=0, tiled=True)]
    reduce_scatter x3, waiting for transfers between devices: 99.8 us -> 65.1 us  [scatter_sum(): lax.psum_scatter(partial.astype(jnp.bfloat16), 'dp', scatter_dimension=0,...]
    all_gather x3, waiting for transfers between devices: 99.8 us -> 84.7 us  [the longest x1 29 us: local(): hidden = lax.all_gather(hidden, 'dp', axis=0, tiled=True)]
    all_to_all x4 -> x2, starting transfers between devices: 18.2 us -> 8.75 us  [bring_back(): lax.all_to_all(sending, BOTH, split_axis=0, concat_axis=0, tiled=True)]
    dot_general x6 -> x8, matrix products: 20.6 us -> 17.8 us  [the longest x1 3.4 us: local(): jnp.einsum('nd,hd->nh', grad_rows, w_down, preferred_element_type=jnp.flo...]
  transfers between devices with their start and end apart: 10 -> 8, of which waited for: 9 -> 7; matrix products, arithmetic and copies ran while one was open for 10% -> 9% of each run, Pallas kernels for 0% -> 0%
where the time goes in v1:
time: 279 us
  waiting for transfers between devices  164 us (59%)
  blocking collectives  53.1 us (19%)
  matrix products  27 us (10%)
  between operations  14.3 us (5%)
  starting transfers between devices  8.99 us (3%)
  local copies, waits for them, and re-layouts  6.95 us (2%)
  other arithmetic  5.03 us (2%)
    reduce_scatter x3, waiting for transfers between devices, scatter_sum(): lax.psum_scatter(partial.astype(jnp.bfloat16), 'dp', scatter_dimension=0,...  65.1 us
    all_to_all x2, blocking collectives, spread(): lax.all_to_all(sending, BOTH, split_axis=0, concat_axis=0, tiled=True)  53.1 us
    all_gather x1, waiting for transfers between devices, local(): hidden = lax.all_gather(hidden, 'dp', axis=0, tiled=True)  29 us
    all_gather x1, waiting for transfers between devices, local(): up_grad_pre = lax.all_gather(up_grad_pre, 'dp', axis=0, tiled=True)  27.9 us
    all_gather x1, waiting for transfers between devices, local(): gate_grad_pre = lax.all_gather(gate_grad_pre, 'dp', axis=0, tiled=True)  27.8 us
    all_to_all x2, waiting for transfers between devices, bring_back(): lax.all_to_all(sending, BOTH, split_axis=0, concat_axis=0, tiled=True)  12.6 us
    all_to_all x2, starting transfers between devices, bring_back(): lax.all_to_all(sending, BOTH, split_axis=0, concat_axis=0, tiled=True)  8.75 us
  transfers between devices with their start and end apart: 8, of which 7 were waited for; matrix products, arithmetic and copies ran while one was open for 9% of the time, Pallas kernels for 0%

profile of v1, /device:TPU:0, one launch (start us, length us, event | category | flops | bytes accessed | tf_op | source)
XLA Modules:
  0.0 278.8 jit_solution(12957339569252015699)
XLA Ops:
  7.2 0.8 fusion.12
  8.0 0.2 reduce_window_sum.11
  8.2 0.8 select_reduce_fusion
  9.1 0.7 multiply_add_fusion
  9.7 1.4 convolution_convert_fusion.1
  11.1 0.5 reshape.42
  11.6 0.1 copy.24
  11.7 29.1 %all_to_all.20 = bf16[32,20,512]{2,1,0:T(8,128)(2,1)S(1)} all-to-all(bf16[32,20,512]{2,1,0:T(8,128)(2,1)S(1)} %bitcast.42), channel_id=1, replica_groups=mesh['dp'=4,'expert'=8] {'dp','expert'}, dimensions={0} | all-to-all | bytes 1310720 | tf_op jit(solution)/shard_map/all_to_all | solution.py:15
  40.8 0.1 reshape.43
  40.9 2.0 convolution_convert_fusion.5
  42.9 0.0 reduce-scatter.6.cloned.1.call-start
  43.0 1.1 copy-done.7
  44.1 2.0 convolution_convert_fusion.4
  46.1 0.0 reduce-scatter.8.cloned.1.call-start
  46.1 1.0 copy-done.3
  47.1 0.4 convolution_convert_fusion
  47.5 0.5 reshape.46
  48.0 0.1 copy.25
  48.1 24.0 %all_to_all.21 = bf16[32,20,512]{2,1,0:T(8,128)(2,1)S(1)} all-to-all(bf16[32,20,512]{2,1,0:T(8,128)(2,1)S(1)} %bitcast.43), channel_id=1, replica_groups=mesh['dp'=4,'expert'=8] {'dp','expert'}, dimensions={0} | all-to-all | bytes 1310720 | tf_op jit(solution)/shard_map/all_to_all | solution.py:15
  72.1 0.1 reshape.47
  72.3 3.4 %convolution_convert_fusion.3 = bf16[640,1024]{1,0:T(8,128)(2,1)} fusion(bf16[640,512]{1,0:T(8,128)(2,1)S(1)} %reshape.47, bf16[1024,512]{1,0:T(8,128)(2,1)} %param.13), kind=kOutput, calls=%fused_computation.5 | convolution fusion | flops 671744000 | bytes 3014656 | tf_op jit(solution)/shard_map/nd,hd->nh/dot_general | solution.py:59
  75.7 0.0 all-gather.6.cloned.1.call-start
  75.8 0.8 reduce-scatter.4.cloned.1.call-done
  76.5 32.1 %reduce-scatter.6.cloned.1.call-done = bf16[160,1024]{1,0:T(8,128)(2,1)} async-done(((bf16[640,1024]{1,0:T(8,128)(2,1)}), bf16[160,1024]{1,0:T(8,128)(2,1)}) %reduce-scatter.6.cloned.1.call-update) | async-done | bytes 327696 | tf_op jit(solution)/shard_map/reduce_scatter | solution.py:32
  108.6 32.3 %reduce-scatter.8.cloned.1.call-done = bf16[160,1024]{1,0:T(8,128)(2,1)} async-done(((bf16[640,1024]{1,0:T(8,128)(2,1)}), bf16[160,1024]{1,0:T(8,128)(2,1)}) %reduce-scatter.8.cloned.1.call-update) | async-done | bytes 327696 | tf_op jit(solution)/shard_map/reduce_scatter | solution.py:32
  140.9 2.5 fusion.5
  143.5 0.5 all-gather.8.cloned.1.call-update
  144.1 0.5 all-gather.4.cloned.1.call-update
  144.7 27.8 %all-gather.6.cloned.1.call-done = bf16[640,1024]{1,0:T(8,128)(2,1)} async-done(((bf16[160,1024]{1,0:T(8,128)(2,1)}), bf16[640,1024]{1,0:T(8,128)(2,1)}) %all-gather.6.cloned.1.call-update) | async-done | bytes 1310736 | tf_op jit(solution)/shard_map/all_gather | solution.py:68
  172.4 3.2 %fusion.17 = f32[640,512]{1,0:T(8,128)} fusion(bf16[640,1024]{1,0:T(8,128)(2,1)} %all-gather.6.cloned.1.call-done, bf16[1024,512]{1,0:T(8,128)(2,1)S(1)} %copy-done), kind=kOutput, calls=%fused_computation.40 | convolution fusion | flops 671088640 | bytes 3670016 | tf_op jit(solution)/shard_map/dot_general | solution.py:74
  175.6 27.9 %all-gather.8.cloned.1.call-done = bf16[640,1024]{1,0:T(8,128)(2,1)} async-done(((bf16[160,1024]{1,0:T(8,128)(2,1)}), bf16[640,1024]{1,0:T(8,128)(2,1)}) %all-gather.8.cloned.1.call-update) | async-done | bytes 1310736 | tf_op jit(solution)/shard_map/all_gather | solution.py:70
  203.5 2.6 fusion.1
  206.1 1.0 reshape.48
  207.1 4.6 %all-to-all-start.3 = ((bf16[32,20,512]{2,1,0:T(8,128)(2,1)}), bf16[32,20,512]{2,1,0:T(8,128)(2,1)S(1)}, u32[]{:S(2)}, u32[]{:S(2)}) async-start(bf16[32,20,512]{2,1,0:T(8,128)(2,1)} %reshape.48), calls=%async_computation.6 | async-start | bytes 1572864 | tf_op jit(solution)/shard_map/all_to_all | solution.py:22
  211.7 29.0 %all-gather.4.cloned.1.call-done = bf16[640,1024]{1,0:T(8,128)(2,1)} async-done(((bf16[160,1024]{1,0:T(8,128)(2,1)}), bf16[640,1024]{1,0:T(8,128)(2,1)}) %all-gather.4.cloned.1.call-update) | async-done | bytes 1310736 | tf_op jit(solution)/shard_map/all_gather | solution.py:64
  240.7 2.5 convolution_convert_fusion.9
  243.2 1.0 reshape.44
  244.2 4.2 %all-to-all-start.1 = ((bf16[32,20,512]{2,1,0:T(8,128)(2,1)}), bf16[32,20,512]{2,1,0:T(8,128)(2,1)S(1)}, u32[]{:S(2)}, u32[]{:S(2)}) async-start(bf16[32,20,512]{2,1,0:T(8,128)(2,1)} %reshape.44), calls=%async_computation.3 | async-start | bytes 1572864 | tf_op jit(solution)/shard_map/all_to_all | solution.py:22
  248.4 3.4 %convolution_convert_fusion.7 = bf16[1024,512]{1,0:T(8,128)(2,1)} fusion(bf16[640,1024]{1,0:T(8,128)(2,1)} %all-gather.8.cloned.1.call-done, bf16[640,512]{1,0:T(8,128)(2,1)S(1)} %reshape.43), kind=kOutput, calls=%fused_computation.9 | convolution fusion | flops 671612928 | bytes 3014656 | tf_op jit(solution)/shard_map/nh,nd->hd/dot_general | solution.py:84
  251.8 2.0 convolution_convert_fusion.8
  253.8 2.0 convolution_convert_fusion.6
  255.8 0.5 copy.23
  256.3 0.1 copy.27
  256.4 1.1 convolution_convert_fusion.2
  257.6 12.6 %all-to-all-done.1 = bf16[32,20,512]{2,1,0:T(8,128)(2,1)S(1)} async-done(((bf16[32,20,512]{2,1,0:T(8,128)(2,1)}), bf16[32,20,512]{2,1,0:T(8,128)(2,1)S(1)}, u32[]{:S(2)}, u32[]{:S(2)}) %all-to-all-start.1) | async-done | bytes 655392 | tf_op jit(solution)/shard_map/all_to_all | solution.py:22
  270.2 0.5 copy.20
  270.7 0.1 copy.26
  270.8 1.1 fusion
  (24 shorter events, 0.2 us)
Async XLA Ops:
  7.2 33.8 %copy-start = (bf16[1024,512]{1,0:T(8,128)(2,1)S(1)}, bf16[1024,512]{1,0:T(8,128)(2,1)}, u32[]{:S(2)}) copy-start(bf16[1024,512]{1,0:T(8,128)(2,1)} %param.11) | copy-start | bytes 3145732
  7.2 69.4 %reduce-scatter.4.cloned.1.call-start = ((), (), s32[]{:S(2)}) async-start(), calls=%async_computation.7 | async-start | bytes 1638400 | tf_op jit(solution)/shard_map/reduce_scatter | solution.py:32
  42.9 1.2 copy-start.7
  42.9 65.7 %reduce-scatter.6.cloned.1.call-start = ((), (), s32[]{:S(2)}) async-start(), calls=%async_computation.8 | async-start | bytes 1638400 | tf_op jit(solution)/shard_map/reduce_scatter | solution.py:32
  46.1 1.0 copy-start.3
  46.1 1.0 copy-start.4
  46.1 94.8 %reduce-scatter.8.cloned.1.call-start = ((), (), s32[]{:S(2)}) async-start(), calls=%async_computation.10 | async-start | bytes 1638400 | tf_op jit(solution)/shard_map/reduce_scatter | solution.py:32
  72.3 3.4 %copy-start.1 = (bf16[640,512]{1,0:T(8,128)(2,1)}, bf16[640,512]{1,0:T(8,128)(2,1)S(1)}, u32[]{:S(2)}) copy-start(bf16[640,512]{1,0:T(8,128)(2,1)S(1)} %reshape.47) | copy-start | bytes 1966084
  75.7 96.7 %all-gather.6.cloned.1.call-start = ((), (), s32[]{:S(2)}) async-start(), calls=%async_computation.11 | async-start | bytes 1638400 | tf_op jit(solution)/shard_map/all_gather | solution.py:68
  143.5 60.0 %all-gather.8.cloned.1.call-start = ((), (), s32[]{:S(2)}) async-start(), calls=%async_computation.12 | async-start | bytes 1638400 | tf_op jit(solution)/shard_map/all_gather | solution.py:70
  144.1 96.7 %all-gather.4.cloned.1.call-start = ((), (), s32[]{:S(2)}) async-start(), calls=%async_computation.9 | async-start | bytes 1638400 | tf_op jit(solution)/shard_map/all_gather | solution.py:64
  144.6 58.9 %copy-start.8 = (bf16[1024,512]{1,0:T(8,128)(2,1)S(1)}, bf16[1024,512]{1,0:T(8,128)(2,1)}, u32[]{:S(2)}) copy-start(bf16[1024,512]{1,0:T(8,128)(2,1)} %param.12) | copy-start | bytes 3145732
  207.1 37.1 %all-to-all-start.3 = ((bf16[32,20,512]{2,1,0:T(8,128)(2,1)}), bf16[32,20,512]{2,1,0:T(8,128)(2,1)S(1)}, u32[]{:S(2)}, u32[]{:S(2)}) async-start(bf16[32,20,512]{2,1,0:T(8,128)(2,1)} %reshape.48), calls=%async_computation.6 | async-start | bytes 1572864 | tf_op jit(solution)/shard_map/all_to_all | solution.py:22
  244.2 26.0 %all-to-all-start.1 = ((bf16[32,20,512]{2,1,0:T(8,128)(2,1)}), bf16[32,20,512]{2,1,0:T(8,128)(2,1)S(1)}, u32[]{:S(2)}, u32[]{:S(2)}) async-start(bf16[32,20,512]{2,1,0:T(8,128)(2,1)} %reshape.44), calls=%async_computation.3 | async-start | bytes 1572864 | tf_op jit(solution)/shard_map/all_to_all | solution.py:22
  248.4 3.4 %copy-start.5 = (bf16[640,1024]{1,0:T(8,128)(2,1)S(1)}, bf16[640,1024]{1,0:T(8,128)(2,1)}, u32[]{:S(2)}) copy-start(bf16[640,1024]{1,0:T(8,128)(2,1)} %all-gather.6.cloned.1.call-done) | copy-start | bytes 3932164
  251.8 2.0 copy-start.2
  251.8 2.0 copy-start.6
Sparse Core Ops, SparseCore 0:
  43.0 33.4 reduce-scatter.3
  79.5 29.1 reduce-scatter.5
  111.6 29.2 reduce-scatter.7
  143.6 28.7 all-gather.5
  174.7 28.7 all-gather.7
  205.8 34.8 all-gather.3

commit v2 on v1

--- a/solution.py
+++ b/solution.py
@@ -1,11 +1,18 @@
+import functools
+
 import jax
 import jax.numpy as jnp
+import numpy as np
 from jax import lax
+from jax.experimental import pallas as pl
+from jax.experimental.pallas import tpu as pltpu
 from jax.sharding import PartitionSpec as P
 
 EXPERTS = 8
 CAP = 20
 BOTH = ("dp", "expert")
+LANES = 128
+MESH = pl.DeviceIdType.MESH
 
 
 def spread(slots, cols, group_size):
@@ -92,9 +99,438 @@
     )
 
 
+def dot_nt(a, b):
+    return lax.dot_general(a, b, (((1,), (1,)), ((), ())), preferred_element_type=jnp.float32)
+
+
+def dot_tn(a, b):
+    return lax.dot_general(a, b, (((0,), (0,)), ((), ())), preferred_element_type=jnp.float32)
+
+
+def dot_nn(a, b):
+    return jnp.dot(a, b, preferred_element_type=jnp.float32)
+
+
+def fused_kernel(
+    n_dp,
+    ids_ref,
+    weight_ref,
+    row_key_ref,
+    lane_key_ref,
+    tokens_ref,
+    cot_ref,
+    w_gate_ref,
+    w_up_ref,
+    w_down_ref,
+    layer_out_ref,
+    token_grad_ref,
+    gate_grad_ref,
+    up_grad_ref,
+    down_grad_ref,
+    slots,
+    rows_in,
+    raw,
+    rows,
+    partial,
+    own_partial,
+    summed_in,
+    hidden_all,
+    back_out,
+    back_in,
+    final,
+    big,
+    pick,
+    spread_send,
+    spread_recv,
+    piece_send,
+    piece_recv,
+    sum_send,
+    sum_recv,
+    hid_send,
+    hid_recv,
+    ret_send,
+    ret_recv,
+    fin_send,
+    fin_recv,
+):
+    n_ex = EXPERTS
+    n_tok = tokens_ref.shape[0]
+    cols = w_gate_ref.shape[1]
+    width = w_gate_ref.shape[0]
+    chunks = cols // LANES
+    block = chunks * CAP
+    group_rows = n_ex * CAP
+    d = lax.axis_index("dp")
+    e = lax.axis_index("expert")
+
+    def dp_at(k):
+        return lax.rem(d + k + n_dp, n_dp)
+
+    def ex_at(k):
+        return lax.rem(e + k + n_ex, n_ex)
+
+    def copy(src, dst, send_sem, recv_sem, to_dp, to_ex):
+        return pltpu.make_async_remote_copy(
+            src_ref=src,
+            dst_ref=dst,
+            send_sem=send_sem,
+            recv_sem=recv_sem,
+            device_id=(to_dp, to_ex),
+            device_id_type=MESH,
+        )
+
+    barrier = pltpu.get_barrier_semaphore()
+    for k in range(1, n_ex):
+        pl.semaphore_signal(barrier, inc=1, device_id=(d, ex_at(k)), device_id_type=MESH)
+    for k in range(1, n_dp):
+        pl.semaphore_signal(barrier, inc=1, device_id=(dp_at(k), e), device_id_type=MESH)
+
+    ids = ids_ref[...]
+    onehot = ids == lax.broadcasted_iota(jnp.int32, (n_ex, n_tok), 0)
+    onehot_f = onehot.astype(jnp.float32)
+    earlier = (
+        lax.broadcasted_iota(jnp.int32, (n_tok, n_tok), 0)
+        < lax.broadcasted_iota(jnp.int32, (n_tok, n_tok), 1)
+    ).astype(jnp.bfloat16)
+    before = dot_nn(onehot_f.astype(jnp.bfloat16), earlier)
+    place = jnp.sum(onehot_f * before, axis=0, keepdims=True).astype(jnp.int32)
+    slot = ids * CAP + place
+    row_key = row_key_ref[...]
+    for c in range(chunks):
+        big[:, c * n_tok : (c + 1) * n_tok] = (
+            (row_key == slot + c * group_rows).astype(jnp.float32).astype(jnp.bfloat16)
+        )
+    lane_key = lane_key_ref[...]
+    for c in range(chunks):
+        want = lax.broadcasted_iota(jnp.int32, (group_rows, 1), 0) + c * group_rows
+        pick[c] = (lane_key == want).astype(jnp.float32).astype(jnp.bfloat16)
+
+    started = []
+
+    def spread(a, source):
+        for j in range(n_dp):
+            stack = jnp.concatenate(
+                [
+                    source[:, j * cols + c * LANES : j * cols + (c + 1) * LANES]
+                    for c in range(chunks)
+                ],
+                axis=0,
+            )
+            placed = dot_nn(big[...], stack).astype(jnp.bfloat16)
+            slots[a, :, :, j * LANES : (j + 1) * LANES] = placed.reshape(n_ex, block, LANES)
+
+    def send_spread(a):
+        for k in range(1, n_ex):
+            to = ex_at(k)
+            cp = copy(
+                slots.at[a, to], rows_in.at[a, e], spread_send.at[a, k], spread_recv.at[a, k], d, to
+            )
+            cp.start()
+            started.append(cp)
+        rows_in[a, e] = slots[a, e]
+
+    spread(0, tokens_ref[...])
+    pl.semaphore_wait(barrier, n_ex - 1 + n_dp - 1)
+    send_spread(0)
+    spread(1, (weight_ref[...] * cot_ref[...].astype(jnp.float32)).astype(jnp.bfloat16))
+    send_spread(1)
+
+    def forward(a):
+        for k in range(n_ex):
+            source = ex_at(-k)
+            if k > 0:
+                copy(
+                    rows_in.at[a, source],
+                    rows_in.at[a, source],
+                    spread_send.at[a, k],
+                    spread_recv.at[a, k],
+                    d,
+                    source,
+                ).wait_recv()
+            for kd in range(1, n_dp):
+                to = dp_at(kd)
+                cp = copy(
+                    rows_in.at[a, source, :, pl.ds(pl.multiple_of(to * LANES, LANES), LANES)],
+                    raw.at[a, kd, source],
+                    piece_send.at[a, kd, k],
+                    piece_recv.at[a, kd, k],
+                    to,
+                    e,
+                )
+                cp.start()
+                started.append(cp)
+        raw[a, 0] = rows_in[a, :, :, pl.ds(pl.multiple_of(d * LANES, LANES), LANES)]
+
+    def arrange(a, kd):
+        if kd > 0:
+            for k in range(n_ex):
+                source = lax.rem(e - k + n_ex, n_ex)
+                copy(
+                    raw.at[a, kd, source],
+                    raw.at[a, kd, source],
+                    piece_send.at[a, kd, k],
+                    piece_recv.at[a, kd, k],
+                    dp_at(-kd),
+                    e,
+                ).wait_recv()
+        arrived = raw[a, kd].reshape(n_ex * block, LANES)
+        for c in range(chunks):
+            rows[a, kd, :, c * LANES : (c + 1) * LANES] = dot_nn(pick[c], arrived).astype(
+                jnp.bfloat16
+            )
+
+    def multiply(m, a, kd, w_ref):
+        value = dot_nt(rows[a, kd], w_ref[...])
+        if kd == 0:
+            own_partial[m] = value
+            return
+        partial[m, kd - 1] = value.astype(jnp.bfloat16)
+        cp = copy(
+            partial.at[m, kd - 1],
+            summed_in.at[m, kd - 1],
+            sum_send.at[m, kd],
+            sum_recv.at[m, kd],
+            dp_at(-kd),
+            e,
+        )
+        cp.start()
+        started.append(cp)
+
+    forward(0)
+    for kd in range(n_dp):
+        arrange(0, kd)
+        multiply(0, 0, kd, w_gate_ref)
+        multiply(1, 0, kd, w_up_ref)
+    forward(1)
+    for kd in range(n_dp):
+        arrange(1, kd)
+        multiply(2, 1, kd, w_down_ref)
+
+    def total(m):
+        for kd in range(1, n_dp):
+            copy(
+                summed_in.at[m, kd - 1],
+                summed_in.at[m, kd - 1],
+                sum_send.at[m, kd],
+                sum_recv.at[m, kd],
+                dp_at(kd),
+                e,
+            ).wait_recv()
+        value = own_partial[m]
+        for kd in range(1, n_dp):
+            value = value + summed_in[m, kd - 1].astype(jnp.float32)
+        return value
+
+    def share(m, value):
+        hidden_all[m, 0] = value
+        for kd in range(1, n_dp):
+            cp = copy(
+                hidden_all.at[m, 0],
+                hidden_all.at[m, kd],
+                hid_send.at[m, kd],
+                hid_recv.at[m, kd],
+                dp_at(kd),
+                e,
+            )
+            cp.start()
+            started.append(cp)
+
+    gate_pre = total(0)
+    sigmoid = 1.0 / (1.0 + jnp.exp(-gate_pre))
+    silu = gate_pre * sigmoid
+    own_partial[0] = silu
+    up_pre = total(1)
+    share(0, (silu * up_pre).astype(jnp.bfloat16))
+    own_partial[1] = up_pre * (sigmoid * (1.0 + gate_pre * (1.0 - sigmoid)))
+    hidden_grad = total(2)
+    share(1, (hidden_grad * own_partial[1]).astype(jnp.bfloat16))
+    share(2, (hidden_grad * own_partial[0]).astype(jnp.bfloat16))
+
+    def wait_hidden(m, kd):
+        if kd > 0:
+            copy(
+                hidden_all.at[m, kd],
+                hidden_all.at[m, kd],
+                hid_send.at[m, kd],
+                hid_recv.at[m, kd],
+                dp_at(-kd),
+                e,
+            ).wait_recv()
+
+    def send_back(b, kd, value):
+        value = value.astype(jnp.bfloat16)
+        back = dot_tn(pick[0], value[:, :LANES])
+        for c in range(1, chunks):
+            back = back + dot_tn(pick[c], value[:, c * LANES : (c + 1) * LANES])
+        back = back.astype(jnp.bfloat16).reshape(n_ex, block, LANES)
+        if kd == 0:
+            back_in[b, 0] = back
+            return
+        back_out[b, kd - 1] = back
+        cp = copy(
+            back_out.at[b, kd - 1],
+            back_in.at[b, kd],
+            ret_send.at[b, kd],
+            ret_recv.at[b, kd],
+            dp_at(-kd),
+            e,
+        )
+        cp.start()
+        started.append(cp)
+
+    def finish_send(b, kd):
+        if kd > 0:
+            copy(
+                back_in.at[b, kd],
+                back_in.at[b, kd],
+                ret_send.at[b, kd],
+                ret_recv.at[b, kd],
+                dp_at(kd),
+                e,
+            ).wait_recv()
+        j = dp_at(kd)
+        for k in range(1, n_ex):
+            to = ex_at(k)
+            cp = copy(
+                back_in.at[b, kd, to],
+                final.at[b, j, e],
+                fin_send.at[b, kd, k],
+                fin_recv.at[b, kd, k],
+                d,
+                to,
+            )
+            cp.start()
+            started.append(cp)
+        final[b, j, e] = back_in[b, kd, e]
+
+    for kd in range(n_dp):
+        wait_hidden(0, kd)
+        send_back(0, kd, dot_nn(hidden_all[0, kd], w_down_ref[...]))
+    for kd in range(n_dp):
+        finish_send(0, kd)
+    for kd in range(n_dp):
+        wait_hidden(1, kd)
+        wait_hidden(2, kd)
+        send_back(
+            1,
+            kd,
+            dot_nn(hidden_all[1, kd], w_gate_ref[...]) + dot_nn(hidden_all[2, kd], w_up_ref[...]),
+        )
+    for kd in range(n_dp):
+        finish_send(1, kd)
+
+    tile = 256 if width % 256 == 0 else width
+    for m, a, out_ref in ((0, 1, down_grad_ref), (1, 0, gate_grad_ref), (2, 0, up_grad_ref)):
+        right = rows[a].reshape(n_dp * group_rows, cols)
+        for t in range(width // tile):
+            left = hidden_all[m, :, :, t * tile : (t + 1) * tile].reshape(n_dp * group_rows, tile)
+            out_ref[t * tile : (t + 1) * tile, :] = dot_tn(left, right).astype(jnp.bfloat16)
+
+    def place_back(b, out_ref):
+        for kd in range(n_dp):
+            for k in range(1, n_ex):
+                source = ex_at(-k)
+                copy(
+                    final.at[b, dp_at(kd), source],
+                    final.at[b, dp_at(kd), source],
+                    fin_send.at[b, kd, k],
+                    fin_recv.at[b, kd, k],
+                    d,
+                    source,
+                ).wait_recv()
+        for j in range(n_dp):
+            value = dot_tn(big[...], final[b, j].reshape(n_ex * block, LANES))
+            for c in range(chunks):
+                piece = value[c * n_tok : (c + 1) * n_tok]
+                if b == 0:
+                    piece = weight_ref[...] * piece
+                out_ref[:, j * cols + c * LANES : j * cols + (c + 1) * LANES] = piece.astype(
+                    jnp.bfloat16
+                )
+
+    place_back(0, layer_out_ref)
+    place_back(1, token_grad_ref)
+    for cp in started:
+        cp.wait_send()
+
+
+def local_fused(tokens, expert_ids, route_weight, cotangent, w_gate, w_up, w_down):
+    n_dp = lax.axis_size("dp")
+    n_ex = lax.axis_size("expert")
+    n_tok, features = tokens.shape
+    width, cols = w_gate.shape
+    chunks = cols // LANES
+    block = chunks * CAP
+    group_rows = n_ex * CAP
+    at = np.arange(n_ex * block)
+    key = (at // block) * CAP + at % CAP + ((at % block) // CAP) * group_rows
+    key = key.astype(np.int32)
+    bf16 = jnp.bfloat16
+    vmem = pl.BlockSpec(memory_space=pltpu.VMEM)
+    dma = pltpu.SemaphoreType.DMA
+    return pl.pallas_call(
+        functools.partial(fused_kernel, n_dp),
+        out_shape=(
+            jax.ShapeDtypeStruct((n_tok, features), bf16),
+            jax.ShapeDtypeStruct((n_tok, features), bf16),
+            jax.ShapeDtypeStruct((width, cols), bf16),
+            jax.ShapeDtypeStruct((width, cols), bf16),
+            jax.ShapeDtypeStruct((width, cols), bf16),
+        ),
+        in_specs=[vmem] * 9,
+        out_specs=(vmem,) * 5,
+        scratch_shapes=[
+            pltpu.VMEM((2, n_ex, block, n_dp * LANES), bf16),
+            pltpu.VMEM((2, n_ex, block, n_dp * LANES), bf16),
+            pltpu.VMEM((2, n_dp, n_ex, block, LANES), bf16),
+            pltpu.VMEM((2, n_dp, group_rows, cols), bf16),
+            pltpu.VMEM((3, n_dp - 1, group_rows, width), bf16),
+            pltpu.VMEM((3, group_rows, width), jnp.float32),
+            pltpu.VMEM((3, n_dp - 1, group_rows, width), bf16),
+            pltpu.VMEM((3, n_dp, group_rows, width), bf16),
+            pltpu.VMEM((2, n_dp - 1, n_ex, block, LANES), bf16),
+            pltpu.VMEM((2, n_dp, n_ex, block, LANES), bf16),
+            pltpu.VMEM((2, n_dp, n_ex, block, LANES), bf16),
+            pltpu.VMEM((n_ex * block, chunks * n_tok), bf16),
+            pltpu.VMEM((chunks, group_rows, n_ex * block), bf16),
+            dma((2, n_ex)),
+            dma((2, n_ex)),
+            dma((2, n_dp, n_ex)),
+            dma((2, n_dp, n_ex)),
+            dma((3, n_dp)),
+            dma((3, n_dp)),
+            dma((3, n_dp)),
+            dma((3, n_dp)),
+            dma((2, n_dp)),
+            dma((2, n_dp)),
+            dma((2, n_dp, n_ex)),
+            dma((2, n_dp, n_ex)),
+        ],
+        compiler_params=pltpu.CompilerParams(
+            collective_id=0, has_side_effects=True, vmem_limit_bytes=56 * 1024 * 1024
+        ),
+        cost_estimate=pl.CostEstimate(
+            flops=18 * n_dp * group_rows * width * cols,
+            bytes_accessed=12 * width * cols + 8 * n_tok * features,
+            transcendentals=group_rows * width,
+        ),
+    )(
+        expert_ids.reshape(1, n_tok),
+        route_weight,
+        jnp.asarray(key)[:, None],
+        jnp.asarray(key)[None, :],
+        tokens,
+        cotangent,
+        w_gate,
+        w_up,
+        w_down,
+    )
+
+
 def solution(mesh):
+    one_block = mesh.shape["expert"] == EXPERTS
     return jax.shard_map(
-        local,
+        local_fused if one_block else local,
         mesh=mesh,
         in_specs=(
             P(BOTH, None),

time: 279 us -> 170 us (0.61)
  waiting for transfers between devices: 164 us -> 0 us
  Pallas kernels: 0 us -> 159 us
  blocking collectives: 53.1 us -> 0 us
  matrix products: 27 us -> 0 us
  between operations: 14.3 us -> 0.66 us
  starting transfers between devices: 8.99 us -> 0 us
  other arithmetic: 5.03 us -> 0 us
    pallas_call x0 -> x1, Pallas kernels: none -> 159 us  [local_fused(): pl.pallas_call(functools.partial(fused_kernel, n_dp), out_shape=(jax.Shap...]
    all_gather x3 -> x0, waiting for transfers between devices: 84.7 us -> none  [the longest x1 29 us: local(): hidden = lax.all_gather(hidden, 'dp', axis=0, tiled=True)]
    reduce_scatter x3 -> x0, waiting for transfers between devices: 65.1 us -> none  [scatter_sum(): lax.psum_scatter(partial.astype(jnp.bfloat16), 'dp', scatter_dimension=0,...]
    all_to_all x2 -> x0, blocking collectives: 53.1 us -> none  [spread(): lax.all_to_all(sending, BOTH, split_axis=0, concat_axis=0, tiled=True)]
    dot_general x13 -> x0, matrix products: 27 us -> none  [the longest x1 3.41 us: local(): jnp.einsum('nh,nd->hd', up_grad_pre, token_rows, preferred_element_type=j...]
    all_to_all x2 -> x0, waiting for transfers between devices: 12.6 us -> none  [bring_back(): lax.all_to_all(sending, BOTH, split_axis=0, concat_axis=0, tiled=True)]
    all_to_all x2 -> x0, starting transfers between devices: 8.75 us -> none  [bring_back(): lax.all_to_all(sending, BOTH, split_axis=0, concat_axis=0, tiled=True)]
    unnamed x20 -> x14, local copies, waits for them, and re-layouts: 2.43 us -> 9.42 us
  transfers between devices with their start and end apart: 8 -> 0, of which waited for: 7 -> 0; matrix products, arithmetic and copies ran while one was open for 9% -> 0% of each run, Pallas kernels for 0% -> 0%
where the time goes in v2:
time: 170 us; the launch traced here: 169 us
  Pallas kernels  159 us (94%)
  local copies, waits for them, and re-layouts  9.42 us (6%)
    pallas_call x1, Pallas kernels, local_fused(): pl.pallas_call(functools.partial(fused_kernel, n_dp), out_shape=(jax.Shap...  159 us
    unnamed x14, local copies, waits for them, and re-layouts  9.42 us

profile of v2, /device:TPU:0, one launch (start us, length us, event | category | flops | bytes accessed | tf_op | source)
XLA Modules:
  0.0 169.3 jit_solution(12708421694708780471)
XLA Ops:
  0.6 0.0 copy-start.3
  0.6 0.6 copy-done.3
  1.3 0.7 copy.13.weight_ref
  2.0 159.3 %shard_map.119 = (bf16[128,2048]{1,0:T(8,128)(2,1)}, bf16[128,2048]{1,0:T(8,128)(2,1)}, bf16[1024,512]{1,0:T(8,128)(2,1)}, bf16[1024,512]{1,0:T(8,128)(2,1)}, bf16[1024,512]{1,0:T(8,128)(2,1)}) custom-call(s32[1,128]{1,0:T(1,128)} %bitcast.1, f32[128,1]{1,0:T(8,128)} %copy.13.weight_ref, s32[640,1]{1,0:T(8,128)} %constant.3.row_key_ref, ...), custom_call_target="tpu_custom_call" | custom-call | flops 6039797760 | bytes 8388608 | tf_op jit(solution)/shard_map/pallas_call | solution.py:471
  161.3 0.0 copy-start.2
  161.3 2.0 %copy.19 = bf16[128,2048]{1,0:T(8,128)(2,1)} copy(bf16[128,2048]{1,0:T(8,128)(2,1)} %get-tuple-element.10) | data formatting | bytes 1048576
  163.3 1.9 %copy.20 = bf16[128,2048]{1,0:T(8,128)(2,1)} copy(bf16[128,2048]{1,0:T(8,128)(2,1)} %get-tuple-element.11) | data formatting | bytes 1048576
  165.2 0.0 copy-done.2
  165.2 0.0 copy-start.1
  165.2 1.0 copy.21
  166.1 0.6 copy-done.1
  166.8 0.0 copy-start
  166.8 1.0 copy.22
  167.7 0.6 copy-done
  168.4 1.0 copy.23
Async XLA Ops:
  0.6 0.7 copy-start.3
  161.3 3.9 %copy-start.2 = (bf16[1024,512]{1,0:T(8,128)(2,1)S(1)}, bf16[1024,512]{1,0:T(8,128)(2,1)}, u32[]{:S(2)}) copy-start(bf16[1024,512]{1,0:T(8,128)(2,1)} %get-tuple-element.12) | copy-start | bytes 3145732
  165.2 1.6 copy-start.1
  166.8 1.6 copy-start

commit v3 on v2

--- a/solution.py
+++ b/solution.py
@@ -122,8 +122,8 @@
     w_gate_ref,
     w_up_ref,
     w_down_ref,
-    layer_out_ref,
-    token_grad_ref,
+    final,
+    big,
     gate_grad_ref,
     up_grad_ref,
     down_grad_ref,
@@ -134,11 +134,10 @@
     partial,
     own_partial,
     summed_in,
+    relayed,
     hidden_all,
     back_out,
     back_in,
-    final,
-    big,
     pick,
     spread_send,
     spread_recv,
@@ -160,11 +159,15 @@
     chunks = cols // LANES
     block = chunks * CAP
     group_rows = n_ex * CAP
+    half = group_rows // 2
     d = lax.axis_index("dp")
     e = lax.axis_index("expert")
 
+    across_x = d + 1 - 2 * lax.rem(d, 2)
+    peers = (d, across_x, lax.rem(d + 2, 4), 3 - d)
+
     def dp_at(k):
-        return lax.rem(d + k + n_dp, n_dp)
+        return peers[k]
 
     def ex_at(k):
         return lax.rem(e + k + n_ex, n_ex)
@@ -270,7 +273,7 @@
                     raw.at[a, kd, source],
                     piece_send.at[a, kd, k],
                     piece_recv.at[a, kd, k],
-                    dp_at(-kd),
+                    dp_at(kd),
                     e,
                 ).wait_recv()
         arrived = raw[a, kd].reshape(n_ex * block, LANES)
@@ -279,22 +282,56 @@
                 jnp.bfloat16
             )
 
+    upper, lower = pl.ds(0, half), pl.ds(half, half)
+
+    def send_sum(m, i, src, to):
+        cp = copy(src, summed_in.at[m, i], sum_send.at[m, i], sum_recv.at[m, i], dp_at(to), e)
+        cp.start()
+        started.append(cp)
+
+    def wait_sum(m, i, source):
+        dst = summed_in.at[m, i]
+        copy(dst, dst, sum_send.at[m, i], sum_recv.at[m, i], dp_at(source), e).wait_recv()
+
     def multiply(m, a, kd, w_ref):
         value = dot_nt(rows[a, kd], w_ref[...])
         if kd == 0:
             own_partial[m] = value
             return
         partial[m, kd - 1] = value.astype(jnp.bfloat16)
-        cp = copy(
-            partial.at[m, kd - 1],
-            summed_in.at[m, kd - 1],
-            sum_send.at[m, kd],
-            sum_recv.at[m, kd],
-            dp_at(-kd),
-            e,
+        if kd == 1:
+            send_sum(m, 0, partial.at[m, 0, upper], 1)
+        elif kd == 2:
+            send_sum(m, 2, partial.at[m, 1, lower], 2)
+        else:
+            send_sum(m, 1, partial.at[m, 2, upper], 1)
+            send_sum(m, 3, partial.at[m, 2, lower], 2)
+
+    def relay_sum(m):
+        wait_sum(m, 1, 1)
+        relayed[m, 0] = (
+            partial[m, 1, :half].astype(jnp.float32) + summed_in[m, 1].astype(jnp.float32)
+        ).astype(jnp.bfloat16)
+        send_sum(m, 4, relayed.at[m, 0], 2)
+        wait_sum(m, 3, 2)
+        relayed[m, 1] = (
+            partial[m, 0, half:].astype(jnp.float32) + summed_in[m, 3].astype(jnp.float32)
+        ).astype(jnp.bfloat16)
+        send_sum(m, 5, relayed.at[m, 1], 1)
+
+    def total(m):
+        wait_sum(m, 0, 1)
+        wait_sum(m, 2, 2)
+        wait_sum(m, 4, 2)
+        wait_sum(m, 5, 1)
+        own = own_partial[m]
+        top = own[:half] + (
+            summed_in[m, 0].astype(jnp.float32) + summed_in[m, 4].astype(jnp.float32)
         )
-        cp.start()
-        started.append(cp)
+        bottom = own[half:] + (
+            summed_in[m, 2].astype(jnp.float32) + summed_in[m, 5].astype(jnp.float32)
+        )
+        return jnp.concatenate([top, bottom], axis=0)
 
     forward(0)
     for kd in range(n_dp):
@@ -302,38 +339,34 @@
         multiply(0, 0, kd, w_gate_ref)
         multiply(1, 0, kd, w_up_ref)
     forward(1)
+    relay_sum(0)
+    relay_sum(1)
     for kd in range(n_dp):
         arrange(1, kd)
         multiply(2, 1, kd, w_down_ref)
 
-    def total(m):
-        for kd in range(1, n_dp):
-            copy(
-                summed_in.at[m, kd - 1],
-                summed_in.at[m, kd - 1],
-                sum_send.at[m, kd],
-                sum_recv.at[m, kd],
-                dp_at(kd),
-                e,
-            ).wait_recv()
-        value = own_partial[m]
-        for kd in range(1, n_dp):
-            value = value + summed_in[m, kd - 1].astype(jnp.float32)
-        return value
+    def send_hidden(m, kd, src, dst, to):
+        cp = copy(src, dst, hid_send.at[m, kd], hid_recv.at[m, kd], dp_at(to), e)
+        cp.start()
+        started.append(cp)
+
+    def await_hidden(m, kd, dst, source):
+        copy(dst, dst, hid_send.at[m, kd], hid_recv.at[m, kd], dp_at(source), e).wait_recv()
 
     def share(m, value):
         hidden_all[m, 0] = value
-        for kd in range(1, n_dp):
-            cp = copy(
-                hidden_all.at[m, 0],
-                hidden_all.at[m, kd],
-                hid_send.at[m, kd],
-                hid_recv.at[m, kd],
-                dp_at(kd),
-                e,
-            )
-            cp.start()
-            started.append(cp)
+        for kd in (1, 2):
+            send_hidden(m, kd, hidden_all.at[m, 0], hidden_all.at[m, kd], kd)
+
+    def relay_hidden(m):
+        await_hidden(m, 1, hidden_all.at[m, 1], 1)
+        send_hidden(m, 3, hidden_all.at[m, 1, lower], hidden_all.at[m, 3, lower], 2)
+        await_hidden(m, 2, hidden_all.at[m, 2], 2)
+        send_hidden(m, 0, hidden_all.at[m, 2, upper], hidden_all.at[m, 3, upper], 1)
+
+    def last_hidden(m):
+        await_hidden(m, 3, hidden_all.at[m, 3, lower], 2)
+        await_hidden(m, 0, hidden_all.at[m, 3, upper], 1)
 
     gate_pre = total(0)
     sigmoid = 1.0 / (1.0 + jnp.exp(-gate_pre))
@@ -342,20 +375,10 @@
     up_pre = total(1)
     share(0, (silu * up_pre).astype(jnp.bfloat16))
     own_partial[1] = up_pre * (sigmoid * (1.0 + gate_pre * (1.0 - sigmoid)))
+    relay_sum(2)
     hidden_grad = total(2)
     share(1, (hidden_grad * own_partial[1]).astype(jnp.bfloat16))
     share(2, (hidden_grad * own_partial[0]).astype(jnp.bfloat16))
-
-    def wait_hidden(m, kd):
-        if kd > 0:
-            copy(
-                hidden_all.at[m, kd],
-                hidden_all.at[m, kd],
-                hid_send.at[m, kd],
-                hid_recv.at[m, kd],
-                dp_at(-kd),
-                e,
-            ).wait_recv()
 
     def send_back(b, kd, value):
         value = value.astype(jnp.bfloat16)
@@ -372,7 +395,7 @@
             back_in.at[b, kd],
             ret_send.at[b, kd],
             ret_recv.at[b, kd],
-            dp_at(-kd),
+            dp_at(kd),
             e,
         )
         cp.start()
@@ -403,21 +426,36 @@
             started.append(cp)
         final[b, j, e] = back_in[b, kd, e]
 
-    for kd in range(n_dp):
-        wait_hidden(0, kd)
+    def output(kd):
         send_back(0, kd, dot_nn(hidden_all[0, kd], w_down_ref[...]))
-    for kd in range(n_dp):
-        finish_send(0, kd)
-    for kd in range(n_dp):
-        wait_hidden(1, kd)
-        wait_hidden(2, kd)
+
+    def input_grad(kd):
         send_back(
             1,
             kd,
             dot_nn(hidden_all[1, kd], w_gate_ref[...]) + dot_nn(hidden_all[2, kd], w_up_ref[...]),
         )
-    for kd in range(n_dp):
-        finish_send(1, kd)
+
+    relay_hidden(0)
+    for kd in (1, 2, 0):
+        output(kd)
+    relay_hidden(1)
+    relay_hidden(2)
+    last_hidden(0)
+    output(3)
+    for kd in (1, 2, 0):
+        input_grad(kd)
+    finish_send(0, 0)
+    finish_send(0, 1)
+    finish_send(0, 2)
+    last_hidden(1)
+    last_hidden(2)
+    input_grad(3)
+    finish_send(1, 0)
+    finish_send(0, 3)
+    finish_send(1, 1)
+    finish_send(1, 2)
+    finish_send(1, 3)
 
     tile = 256 if width % 256 == 0 else width
     for m, a, out_ref in ((0, 1, down_grad_ref), (1, 0, gate_grad_ref), (2, 0, up_grad_ref)):
@@ -426,7 +464,7 @@
             left = hidden_all[m, :, :, t * tile : (t + 1) * tile].reshape(n_dp * group_rows, tile)
             out_ref[t * tile : (t + 1) * tile, :] = dot_tn(left, right).astype(jnp.bfloat16)
 
-    def place_back(b, out_ref):
+    for b in range(2):
         for kd in range(n_dp):
             for k in range(1, n_ex):
                 source = ex_at(-k)
@@ -438,8 +476,37 @@
                     d,
                     source,
                 ).wait_recv()
+    for cp in started:
+        cp.wait_send()
+
+
+def finish_kernel(
+    weight_ref,
+    big_ref,
+    final_ref,
+    gate_in,
+    up_in,
+    down_in,
+    layer_out_ref,
+    token_grad_ref,
+    gate_out,
+    up_out,
+    down_out,
+    sems,
+):
+    copies = [
+        pltpu.make_async_copy(src, dst, sems.at[i])
+        for i, (src, dst) in enumerate(((gate_in, gate_out), (up_in, up_out), (down_in, down_out)))
+    ]
+    for cp in copies:
+        cp.start()
+    n_tok = weight_ref.shape[0]
+    n_dp = final_ref.shape[1]
+    chunks = big_ref.shape[1] // n_tok
+    cols = chunks * LANES
+    for b, out_ref in ((0, layer_out_ref), (1, token_grad_ref)):
         for j in range(n_dp):
-            value = dot_tn(big[...], final[b, j].reshape(n_ex * block, LANES))
+            value = dot_tn(big_ref[...], final_ref[b, j].reshape(big_ref.shape[0], LANES))
             for c in range(chunks):
                 piece = value[c * n_tok : (c + 1) * n_tok]
                 if b == 0:
@@ -447,11 +514,8 @@
                 out_ref[:, j * cols + c * LANES : j * cols + (c + 1) * LANES] = piece.astype(
                     jnp.bfloat16
                 )
-
-    place_back(0, layer_out_ref)
-    place_back(1, token_grad_ref)
-    for cp in started:
-        cp.wait_send()
+    for cp in copies:
+        cp.wait()
 
 
 def local_fused(tokens, expert_ids, route_weight, cotangent, w_gate, w_up, w_down):
@@ -468,14 +532,17 @@
     bf16 = jnp.bfloat16
     vmem = pl.BlockSpec(memory_space=pltpu.VMEM)
     dma = pltpu.SemaphoreType.DMA
-    return pl.pallas_call(
+    vmem_limit = 56 * 1024 * 1024
+    weight_struct = jax.ShapeDtypeStruct((width, cols), bf16)
+    token_struct = jax.ShapeDtypeStruct((n_tok, features), bf16)
+    final, big, gate_grad, up_grad, down_grad = pl.pallas_call(
         functools.partial(fused_kernel, n_dp),
         out_shape=(
-            jax.ShapeDtypeStruct((n_tok, features), bf16),
-            jax.ShapeDtypeStruct((n_tok, features), bf16),
-            jax.ShapeDtypeStruct((width, cols), bf16),
-            jax.ShapeDtypeStruct((width, cols), bf16),
-            jax.ShapeDtypeStruct((width, cols), bf16),
+            jax.ShapeDtypeStruct((2, n_dp, n_ex, block, LANES), bf16),
+            jax.ShapeDtypeStruct((n_ex * block, chunks * n_tok), bf16),
+            weight_struct,
+            weight_struct,
+            weight_struct,
         ),
         in_specs=[vmem] * 9,
         out_specs=(vmem,) * 5,
@@ -486,19 +553,18 @@
             pltpu.VMEM((2, n_dp, group_rows, cols), bf16),
             pltpu.VMEM((3, n_dp - 1, group_rows, width), bf16),
             pltpu.VMEM((3, group_rows, width), jnp.float32),
-            pltpu.VMEM((3, n_dp - 1, group_rows, width), bf16),
+            pltpu.VMEM((3, 6, group_rows // 2, width), bf16),
+            pltpu.VMEM((3, 2, group_rows // 2, width), bf16),
             pltpu.VMEM((3, n_dp, group_rows, width), bf16),
             pltpu.VMEM((2, n_dp - 1, n_ex, block, LANES), bf16),
             pltpu.VMEM((2, n_dp, n_ex, block, LANES), bf16),
-            pltpu.VMEM((2, n_dp, n_ex, block, LANES), bf16),
-            pltpu.VMEM((n_ex * block, chunks * n_tok), bf16),
             pltpu.VMEM((chunks, group_rows, n_ex * block), bf16),
             dma((2, n_ex)),
             dma((2, n_ex)),
             dma((2, n_dp, n_ex)),
             dma((2, n_dp, n_ex)),
-            dma((3, n_dp)),
-            dma((3, n_dp)),
+            dma((3, 6)),
+            dma((3, 6)),
             dma((3, n_dp)),
             dma((3, n_dp)),
             dma((2, n_dp)),
@@ -507,7 +573,7 @@
             dma((2, n_dp, n_ex)),
         ],
         compiler_params=pltpu.CompilerParams(
-            collective_id=0, has_side_effects=True, vmem_limit_bytes=56 * 1024 * 1024
+            collective_id=0, has_side_effects=True, vmem_limit_bytes=vmem_limit
         ),
         cost_estimate=pl.CostEstimate(
             flops=18 * n_dp * group_rows * width * cols,
@@ -525,10 +591,19 @@
         w_up,
         w_down,
     )
+    hbm = pl.BlockSpec(memory_space=pl.ANY)
+    return pl.pallas_call(
+        finish_kernel,
+        out_shape=(token_struct, token_struct, weight_struct, weight_struct, weight_struct),
+        in_specs=[vmem] * 3 + [hbm] * 3,
+        out_specs=(vmem,) * 2 + (hbm,) * 3,
+        scratch_shapes=[dma((3,))],
+        compiler_params=pltpu.CompilerParams(vmem_limit_bytes=vmem_limit),
+    )(route_weight, big, final, gate_grad, up_grad, down_grad)
 
 
 def solution(mesh):
-    one_block = mesh.shape["expert"] == EXPERTS
+    one_block = mesh.shape["expert"] == EXPERTS and mesh.shape["dp"] == 4
     return jax.shard_map(
         local_fused if one_block else local,
         mesh=mesh,

time: 170 us -> 236 us (1.39)
  Pallas kernels: 159 us -> 232 us
  local copies, waits for them, and re-layouts: 9.42 us -> 1.4 us
    pallas_call x0 -> x1, Pallas kernels: none -> 98.9 us  [local_fused(): pl.pallas_call(finish_kernel, out_shape=(token_struct, token_struct, weig...]
    pallas_call x1, Pallas kernels: 159 us -> 133 us  [local_fused(): pl.pallas_call(functools.partial(fused_kernel, n_dp), out_shape=(jax.Shap...]
    unnamed x14 -> x1, local copies, waits for them, and re-layouts: 9.42 us -> 1.4 us
where the time goes in v3:
time: 236 us; the launch traced here: 234 us
  Pallas kernels  232 us (98%)
    pallas_call x1, Pallas kernels, local_fused(): pl.pallas_call(functools.partial(fused_kernel, n_dp), out_shape=(jax.Shap...  133 us
    pallas_call x1, Pallas kernels, local_fused(): pl.pallas_call(finish_kernel, out_shape=(token_struct, token_struct, weig...  98.9 us

profile of v3, /device:TPU:0, one launch (start us, length us, event | category | flops | bytes accessed | tf_op | source)
XLA Modules:
  0.0 233.8 jit_solution(10672132318403492814)
XLA Ops:
  0.6 1.4 copy.14.weight_ref
  2.0 132.7 %shard_map.119 = (bf16[2,4,8,80,128]{4,3,2,1,0:T(8,128)(2,1)}, bf16[640,512]{1,0:T(8,128)(2,1)}, bf16[1024,512]{1,0:T(8,128)(2,1)}, bf16[1024,512]{1,0:T(8,128)(2,1)}, bf16[1024,512]{1,0:T(8,128)(2,1)}) custom-call(s32[1,128]{1,0:T(1,128)} %bitcast.1, f32[128,1]{1,0:T(8,128)} %copy.14.weight_ref, s32[640,1]{1,0:T(8,128)} %constant.3.row_key_ref, ...), custom_call_target="tpu_custom_call" | custom-call | flops 6039797760 | bytes 8388608 | tf_op jit(solution)/shard_map/pallas_call | solution.py:538
  134.7 98.9 %shard_map.120 = (bf16[128,2048]{1,0:T(8,128)(2,1)}, bf16[128,2048]{1,0:T(8,128)(2,1)}, bf16[1024,512]{1,0:T(8,128)(2,1)}, bf16[1024,512]{1,0:T(8,128)(2,1)}, bf16[1024,512]{1,0:T(8,128)(2,1)}) custom-call(f32[128,1]{1,0:T(8,128)} %copy.14.weight_ref, bf16[640,512]{1,0:T(8,128)(2,1)} %get-tuple-element.10.big_ref, ...), custom_call_target="tpu_custom_call" | custom-call | tf_op jit(solution)/shard_map/pallas_call | solution.py:595

commit v4 on v3

--- a/solution.py
+++ b/solution.py
@@ -128,7 +128,7 @@
     up_grad_ref,
     down_grad_ref,
     slots,
-    rows_in,
+    pieces,
     raw,
     rows,
     partial,
@@ -220,62 +220,59 @@
                 axis=0,
             )
             placed = dot_nn(big[...], stack).astype(jnp.bfloat16)
-            slots[a, :, :, j * LANES : (j + 1) * LANES] = placed.reshape(n_ex, block, LANES)
-
-    def send_spread(a):
+            slots[a, j] = placed.reshape(n_ex, block, LANES)
+
+    def send_pieces(a):
+        for kd in range(1, n_dp):
+            to = dp_at(kd)
+            cp = copy(
+                slots.at[a, to],
+                pieces.at[a, kd - 1],
+                spread_send.at[a, kd],
+                spread_recv.at[a, kd],
+                to,
+                e,
+            )
+            cp.start()
+            started.append(cp)
+
+    def forward(a, kd):
+        if kd > 0:
+            dst = pieces.at[a, kd - 1]
+            copy(
+                dst, dst, spread_send.at[a, kd], spread_recv.at[a, kd], dp_at(kd), e
+            ).wait_recv()
+            held = pieces.at[a, kd - 1]
+        else:
+            held = slots.at[a, d]
         for k in range(1, n_ex):
             to = ex_at(k)
             cp = copy(
-                slots.at[a, to], rows_in.at[a, e], spread_send.at[a, k], spread_recv.at[a, k], d, to
+                held.at[to],
+                raw.at[a, kd, e],
+                piece_send.at[a, kd, k],
+                piece_recv.at[a, kd, k],
+                d,
+                to,
             )
             cp.start()
             started.append(cp)
-        rows_in[a, e] = slots[a, e]
+        raw[a, kd, e] = held[e]
 
     spread(0, tokens_ref[...])
     pl.semaphore_wait(barrier, n_ex - 1 + n_dp - 1)
-    send_spread(0)
+    send_pieces(0)
+    forward(0, 0)
     spread(1, (weight_ref[...] * cot_ref[...].astype(jnp.float32)).astype(jnp.bfloat16))
-    send_spread(1)
-
-    def forward(a):
-        for k in range(n_ex):
+    send_pieces(1)
+
+    def arrange(a, kd):
+        for k in range(1, n_ex):
             source = ex_at(-k)
-            if k > 0:
-                copy(
-                    rows_in.at[a, source],
-                    rows_in.at[a, source],
-                    spread_send.at[a, k],
-                    spread_recv.at[a, k],
-                    d,
-                    source,
-                ).wait_recv()
-            for kd in range(1, n_dp):
-                to = dp_at(kd)
-                cp = copy(
-                    rows_in.at[a, source, :, pl.ds(pl.multiple_of(to * LANES, LANES), LANES)],
-                    raw.at[a, kd, source],
-                    piece_send.at[a, kd, k],
-                    piece_recv.at[a, kd, k],
-                    to,
-                    e,
-                )
-                cp.start()
-                started.append(cp)
-        raw[a, 0] = rows_in[a, :, :, pl.ds(pl.multiple_of(d * LANES, LANES), LANES)]
-
-    def arrange(a, kd):
-        if kd > 0:
-            for k in range(n_ex):
-                source = lax.rem(e - k + n_ex, n_ex)
-                copy(
-                    raw.at[a, kd, source],
-                    raw.at[a, kd, source],
-                    piece_send.at[a, kd, k],
-                    piece_recv.at[a, kd, k],
-                    dp_at(kd),
-                    e,
-                ).wait_recv()
+            dst = raw.at[a, kd, source]
+            copy(
+                dst, dst, piece_send.at[a, kd, k], piece_recv.at[a, kd, k], d, source
+            ).wait_recv()
         arrived = raw[a, kd].reshape(n_ex * block, LANES)
         for c in range(chunks):
             rows[a, kd, :, c * LANES : (c + 1) * LANES] = dot_nn(pick[c], arrived).astype(
@@ -333,12 +330,17 @@
         )
         return jnp.concatenate([top, bottom], axis=0)
 
-    forward(0)
+    forward(0, 1)
+    forward(0, 2)
+    forward(0, 3)
+    forward(1, 0)
     for kd in range(n_dp):
         arrange(0, kd)
         multiply(0, 0, kd, w_gate_ref)
         multiply(1, 0, kd, w_up_ref)
-    forward(1)
+        if kd == 0:
+            for other in range(1, n_dp):
+                forward(1, other)
     relay_sum(0)
     relay_sum(1)
     for kd in range(n_dp):
@@ -436,33 +438,37 @@
             dot_nn(hidden_all[1, kd], w_gate_ref[...]) + dot_nn(hidden_all[2, kd], w_up_ref[...]),
         )
 
+    tile = 256 if width % 256 == 0 else width
+
+    def weight_grad(m, a, out_ref):
+        right = rows[a].reshape(n_dp * group_rows, cols)
+        for t in range(width // tile):
+            left = hidden_all[m, :, :, t * tile : (t + 1) * tile].reshape(n_dp * group_rows, tile)
+            out_ref[t * tile : (t + 1) * tile, :] = dot_tn(left, right).astype(jnp.bfloat16)
+
     relay_hidden(0)
     for kd in (1, 2, 0):
         output(kd)
+    finish_send(0, 0)
     relay_hidden(1)
     relay_hidden(2)
     last_hidden(0)
     output(3)
+    finish_send(0, 1)
+    finish_send(0, 2)
     for kd in (1, 2, 0):
         input_grad(kd)
-    finish_send(0, 0)
-    finish_send(0, 1)
-    finish_send(0, 2)
+    finish_send(1, 0)
+    finish_send(0, 3)
+    weight_grad(0, 1, down_grad_ref)
     last_hidden(1)
     last_hidden(2)
     input_grad(3)
-    finish_send(1, 0)
-    finish_send(0, 3)
     finish_send(1, 1)
     finish_send(1, 2)
+    weight_grad(1, 0, gate_grad_ref)
     finish_send(1, 3)
-
-    tile = 256 if width % 256 == 0 else width
-    for m, a, out_ref in ((0, 1, down_grad_ref), (1, 0, gate_grad_ref), (2, 0, up_grad_ref)):
-        right = rows[a].reshape(n_dp * group_rows, cols)
-        for t in range(width // tile):
-            left = hidden_all[m, :, :, t * tile : (t + 1) * tile].reshape(n_dp * group_rows, tile)
-            out_ref[t * tile : (t + 1) * tile, :] = dot_tn(left, right).astype(jnp.bfloat16)
+    weight_grad(2, 0, up_grad_ref)
 
     for b in range(2):
         for kd in range(n_dp):
@@ -492,13 +498,19 @@
     gate_out,
     up_out,
     down_out,
-    sems,
+    held,
+    in_sems,
+    out_sems,
 ):
-    copies = [
-        pltpu.make_async_copy(src, dst, sems.at[i])
-        for i, (src, dst) in enumerate(((gate_in, gate_out), (up_in, up_out), (down_in, down_out)))
+    loads = [
+        pltpu.make_async_copy(src, held.at[i], in_sems.at[i])
+        for i, src in enumerate((gate_in, up_in, down_in))
     ]
-    for cp in copies:
+    stores = [
+        pltpu.make_async_copy(held.at[i], dst, out_sems.at[i])
+        for i, dst in enumerate((gate_out, up_out, down_out))
+    ]
+    for cp in loads:
         cp.start()
     n_tok = weight_ref.shape[0]
     n_dp = final_ref.shape[1]
@@ -514,7 +526,10 @@
                 out_ref[:, j * cols + c * LANES : j * cols + (c + 1) * LANES] = piece.astype(
                     jnp.bfloat16
                 )
-    for cp in copies:
+            if b == 0 and j < len(loads):
+                loads[j].wait()
+                stores[j].start()
+    for cp in stores:
         cp.wait()
 
 
@@ -547,8 +562,8 @@
         in_specs=[vmem] * 9,
         out_specs=(vmem,) * 5,
         scratch_shapes=[
-            pltpu.VMEM((2, n_ex, block, n_dp * LANES), bf16),
-            pltpu.VMEM((2, n_ex, block, n_dp * LANES), bf16),
+            pltpu.VMEM((2, n_dp, n_ex, block, LANES), bf16),
+            pltpu.VMEM((2, n_dp - 1, n_ex, block, LANES), bf16),
             pltpu.VMEM((2, n_dp, n_ex, block, LANES), bf16),
             pltpu.VMEM((2, n_dp, group_rows, cols), bf16),
             pltpu.VMEM((3, n_dp - 1, group_rows, width), bf16),
@@ -559,8 +574,8 @@
             pltpu.VMEM((2, n_dp - 1, n_ex, block, LANES), bf16),
             pltpu.VMEM((2, n_dp, n_ex, block, LANES), bf16),
             pltpu.VMEM((chunks, group_rows, n_ex * block), bf16),
-            dma((2, n_ex)),
-            dma((2, n_ex)),
+            dma((2, n_dp)),
+            dma((2, n_dp)),
             dma((2, n_dp, n_ex)),
             dma((2, n_dp, n_ex)),
             dma((3, 6)),
@@ -597,7 +612,7 @@
         out_shape=(token_struct, token_struct, weight_struct, weight_struct, weight_struct),
         in_specs=[vmem] * 3 + [hbm] * 3,
         out_specs=(vmem,) * 2 + (hbm,) * 3,
-        scratch_shapes=[dma((3,))],
+        scratch_shapes=[pltpu.VMEM((3, width, cols), bf16), dma((3,)), dma((3,))],
         compiler_params=pltpu.CompilerParams(vmem_limit_bytes=vmem_limit),
     )(route_weight, big, final, gate_grad, up_grad, down_grad)
 

time: 236 us -> 128 us (0.54); the launches traced: 234 us -> 128 us
  Pallas kernels: 232 us -> 126 us
    pallas_call x1, Pallas kernels: 98.9 us -> 5.83 us  [local_fused(): pl.pallas_call(finish_kernel, out_shape=(token_struct, token_struct, weig...]
    pallas_call x1, Pallas kernels: 133 us -> 120 us  [local_fused(): pl.pallas_call(functools.partial(fused_kernel, n_dp), out_shape=(jax.Shap...]
where the time goes in v4:
time: 128 us
  Pallas kernels  126 us (98%)
  local copies, waits for them, and re-layouts  1.4 us (1%)
    pallas_call x1, Pallas kernels, local_fused(): pl.pallas_call(functools.partial(fused_kernel, n_dp), out_shape=(jax.Shap...  120 us
    pallas_call x1, Pallas kernels, local_fused(): pl.pallas_call(finish_kernel, out_shape=(token_struct, token_struct, weig...  5.83 us

profile of v4, /device:TPU:0, one launch (start us, length us, event | category | flops | bytes accessed | tf_op | source)
XLA Modules:
  0.0 128.3 jit_solution(478120398281068805)
XLA Ops:
  0.6 1.4 %copy.14.weight_ref = f32[128,1]{1,0:T(8,128)} copy(f32[128,1]{0,1:T(1,128)} %param.10) | data formatting | bytes 1024 | tf_op args[2]
  2.0 120.2 %shard_map.119 = (bf16[2,4,8,80,128]{4,3,2,1,0:T(8,128)(2,1)}, bf16[640,512]{1,0:T(8,128)(2,1)}, bf16[1024,512]{1,0:T(8,128)(2,1)}, bf16[1024,512]{1,0:T(8,128)(2,1)}, bf16[1024,512]{1,0:T(8,128)(2,1)}) custom-call(s32[1,128]{1,0:T(1,128)} %bitcast.1, f32[128,1]{1,0:T(8,128)} %copy.14.weight_ref, s32[640,1]{1,0:T(8,128)} %constant.3.row_key_ref, ...), custom_call_target="tpu_custom_call" | custom-call | flops 6039797760 | bytes 8388608 | tf_op jit(solution)/shard_map/pallas_call | solution.py:553
  122.3 5.8 %shard_map.120 = (bf16[128,2048]{1,0:T(8,128)(2,1)}, bf16[128,2048]{1,0:T(8,128)(2,1)}, bf16[1024,512]{1,0:T(8,128)(2,1)}, bf16[1024,512]{1,0:T(8,128)(2,1)}, bf16[1024,512]{1,0:T(8,128)(2,1)}) custom-call(f32[128,1]{1,0:T(8,128)} %copy.14.weight_ref, bf16[640,512]{1,0:T(8,128)(2,1)} %get-tuple-element.10.big_ref, ...), custom_call_target="tpu_custom_call" | custom-call | tf_op jit(solution)/shard_map/pallas_call | solution.py:610

commit v5 on v4

--- a/solution.py
+++ b/solution.py
@@ -111,6 +111,12 @@
     return jnp.dot(a, b, preferred_element_type=jnp.float32)
 
 
+def weight_column(row):
+    n = row.shape[1]
+    same = lax.broadcasted_iota(jnp.int32, (n, n), 0) == lax.broadcasted_iota(jnp.int32, (n, n), 1)
+    return jnp.sum(jnp.where(same, row, 0.0), axis=1, keepdims=True)
+
+
 def fused_kernel(
     n_dp,
     ids_ref,
@@ -119,11 +125,18 @@
     lane_key_ref,
     tokens_ref,
     cot_ref,
+    w_gate_in,
+    w_up_in,
+    w_down_in,
+    final,
+    big_t,
+    gate_grad_out,
+    up_grad_out,
+    down_grad_out,
+    big,
     w_gate_ref,
     w_up_ref,
     w_down_ref,
-    final,
-    big,
     gate_grad_ref,
     up_grad_ref,
     down_grad_ref,
@@ -138,7 +151,8 @@
     hidden_all,
     back_out,
     back_in,
-    pick,
+    gather,
+    ungather,
     spread_send,
     spread_recv,
     piece_send,
@@ -151,11 +165,21 @@
     ret_recv,
     fin_send,
     fin_recv,
+    load_sem,
+    store_sem,
 ):
+    loads = [
+        pltpu.make_async_copy(src, dst, load_sem.at[i])
+        for i, (src, dst) in enumerate(
+            ((w_gate_in, w_gate_ref), (w_up_in, w_up_ref), (w_down_in, w_down_ref))
+        )
+    ]
+    for cp in loads:
+        cp.start()
     n_ex = EXPERTS
     n_tok = tokens_ref.shape[0]
-    cols = w_gate_ref.shape[1]
-    width = w_gate_ref.shape[0]
+    cols = w_gate_in.shape[1]
+    width = w_gate_in.shape[0]
     chunks = cols // LANES
     block = chunks * CAP
     group_rows = n_ex * CAP
@@ -203,24 +227,25 @@
         big[:, c * n_tok : (c + 1) * n_tok] = (
             (row_key == slot + c * group_rows).astype(jnp.float32).astype(jnp.bfloat16)
         )
-    lane_key = lane_key_ref[...]
-    for c in range(chunks):
-        want = lax.broadcasted_iota(jnp.int32, (group_rows, 1), 0) + c * group_rows
-        pick[c] = (lane_key == want).astype(jnp.float32).astype(jnp.bfloat16)
-
     started = []
 
     def spread(a, source):
+        stack = jnp.concatenate(
+            [
+                jnp.concatenate(
+                    [
+                        source[:, j * cols + c * LANES : j * cols + (c + 1) * LANES]
+                        for j in range(n_dp)
+                    ],
+                    axis=1,
+                )
+                for c in range(chunks)
+            ],
+            axis=0,
+        )
+        placed = dot_nn(big[...], stack).astype(jnp.bfloat16)
         for j in range(n_dp):
-            stack = jnp.concatenate(
-                [
-                    source[:, j * cols + c * LANES : j * cols + (c + 1) * LANES]
-                    for c in range(chunks)
-                ],
-                axis=0,
-            )
-            placed = dot_nn(big[...], stack).astype(jnp.bfloat16)
-            slots[a, j] = placed.reshape(n_ex, block, LANES)
+            slots[a, j] = placed[:, j * LANES : (j + 1) * LANES].reshape(n_ex, block, LANES)
 
     def send_pieces(a):
         for kd in range(1, n_dp):
@@ -263,8 +288,19 @@
     pl.semaphore_wait(barrier, n_ex - 1 + n_dp - 1)
     send_pieces(0)
     forward(0, 0)
-    spread(1, (weight_ref[...] * cot_ref[...].astype(jnp.float32)).astype(jnp.bfloat16))
+    weight = weight_column(weight_ref[...])
+    spread(1, (weight * cot_ref[...].astype(jnp.float32)).astype(jnp.bfloat16))
     send_pieces(1)
+    lane_key = lane_key_ref[...]
+    total_rows = n_ex * block
+    want = lax.broadcasted_iota(jnp.int32, (total_rows, 1), 0)
+    gather[...] = (lane_key == want).astype(jnp.float32).astype(jnp.bfloat16)
+    want = lax.broadcasted_iota(jnp.int32, (1, total_rows), 1)
+    ungather[...] = (row_key == want).astype(jnp.float32).astype(jnp.bfloat16)
+
+    big_t[...] = big[...].T
+    for cp in loads:
+        cp.wait()
 
     def arrange(a, kd):
         for k in range(1, n_ex):
@@ -274,10 +310,11 @@
                 dst, dst, piece_send.at[a, kd, k], piece_recv.at[a, kd, k], d, source
             ).wait_recv()
         arrived = raw[a, kd].reshape(n_ex * block, LANES)
+        ordered = dot_nn(gather[...], arrived).astype(jnp.bfloat16)
         for c in range(chunks):
-            rows[a, kd, :, c * LANES : (c + 1) * LANES] = dot_nn(pick[c], arrived).astype(
-                jnp.bfloat16
-            )
+            rows[a, kd, :, c * LANES : (c + 1) * LANES] = ordered[
+                c * group_rows : (c + 1) * group_rows
+            ]
 
     upper, lower = pl.ds(0, half), pl.ds(half, half)
 
@@ -384,10 +421,10 @@
 
     def send_back(b, kd, value):
         value = value.astype(jnp.bfloat16)
-        back = dot_tn(pick[0], value[:, :LANES])
-        for c in range(1, chunks):
-            back = back + dot_tn(pick[c], value[:, c * LANES : (c + 1) * LANES])
-        back = back.astype(jnp.bfloat16).reshape(n_ex, block, LANES)
+        stack = jnp.concatenate(
+            [value[:, c * LANES : (c + 1) * LANES] for c in range(chunks)], axis=0
+        )
+        back = dot_nn(ungather[...], stack).astype(jnp.bfloat16).reshape(n_ex, block, LANES)
         if kd == 0:
             back_in[b, 0] = back
             return
@@ -440,11 +477,16 @@
 
     tile = 256 if width % 256 == 0 else width
 
-    def weight_grad(m, a, out_ref):
+    stores = []
+
+    def weight_grad(m, a, out_ref, hbm_ref):
         right = rows[a].reshape(n_dp * group_rows, cols)
         for t in range(width // tile):
             left = hidden_all[m, :, :, t * tile : (t + 1) * tile].reshape(n_dp * group_rows, tile)
             out_ref[t * tile : (t + 1) * tile, :] = dot_tn(left, right).astype(jnp.bfloat16)
+        cp = pltpu.make_async_copy(out_ref, hbm_ref, store_sem.at[m])
+        cp.start()
+        stores.append(cp)
 
     relay_hidden(0)
     for kd in (1, 2, 0):
@@ -460,15 +502,15 @@
         input_grad(kd)
     finish_send(1, 0)
     finish_send(0, 3)
-    weight_grad(0, 1, down_grad_ref)
     last_hidden(1)
     last_hidden(2)
     input_grad(3)
     finish_send(1, 1)
     finish_send(1, 2)
-    weight_grad(1, 0, gate_grad_ref)
+    weight_grad(0, 1, down_grad_ref, down_grad_out)
     finish_send(1, 3)
-    weight_grad(2, 0, up_grad_ref)
+    weight_grad(1, 0, gate_grad_ref, gate_grad_out)
+    weight_grad(2, 0, up_grad_ref, up_grad_out)
 
     for b in range(2):
         for kd in range(n_dp):
@@ -484,6 +526,8 @@
                 ).wait_recv()
     for cp in started:
         cp.wait_send()
+    for cp in stores:
+        cp.wait()
 
 
 def finish_kernel(
@@ -512,23 +556,29 @@
     ]
     for cp in loads:
         cp.start()
-    n_tok = weight_ref.shape[0]
+    n_tok = weight_ref.shape[1]
     n_dp = final_ref.shape[1]
-    chunks = big_ref.shape[1] // n_tok
+    chunks = big_ref.shape[0] // n_tok
     cols = chunks * LANES
+    weight = weight_column(weight_ref[...])
     for b, out_ref in ((0, layer_out_ref), (1, token_grad_ref)):
-        for j in range(n_dp):
-            value = dot_tn(big_ref[...], final_ref[b, j].reshape(big_ref.shape[0], LANES))
-            for c in range(chunks):
-                piece = value[c * n_tok : (c + 1) * n_tok]
-                if b == 0:
-                    piece = weight_ref[...] * piece
-                out_ref[:, j * cols + c * LANES : j * cols + (c + 1) * LANES] = piece.astype(
-                    jnp.bfloat16
-                )
-            if b == 0 and j < len(loads):
-                loads[j].wait()
-                stores[j].start()
+        slots = jnp.concatenate(
+            [final_ref[b, j].reshape(big_ref.shape[1], LANES) for j in range(n_dp)], axis=1
+        )
+        value = dot_nn(big_ref[...], slots)
+        for c in range(chunks):
+            piece = value[c * n_tok : (c + 1) * n_tok]
+            if b == 0:
+                piece = weight * piece
+            piece = piece.astype(jnp.bfloat16)
+            for j in range(n_dp):
+                out_ref[:, j * cols + c * LANES : j * cols + (c + 1) * LANES] = piece[
+                    :, j * LANES : (j + 1) * LANES
+                ]
+        if b == 0:
+            for load, store in zip(loads, stores):
+                load.wait()
+                store.start()
     for cp in stores:
         cp.wait()
 
@@ -546,22 +596,26 @@
     key = key.astype(np.int32)
     bf16 = jnp.bfloat16
     vmem = pl.BlockSpec(memory_space=pltpu.VMEM)
+    hbm = pl.BlockSpec(memory_space=pl.ANY)
     dma = pltpu.SemaphoreType.DMA
+    weight_row = route_weight.reshape(1, n_tok)
     vmem_limit = 56 * 1024 * 1024
     weight_struct = jax.ShapeDtypeStruct((width, cols), bf16)
     token_struct = jax.ShapeDtypeStruct((n_tok, features), bf16)
-    final, big, gate_grad, up_grad, down_grad = pl.pallas_call(
+    final, big_t, gate_grad, up_grad, down_grad = pl.pallas_call(
         functools.partial(fused_kernel, n_dp),
         out_shape=(
             jax.ShapeDtypeStruct((2, n_dp, n_ex, block, LANES), bf16),
-            jax.ShapeDtypeStruct((n_ex * block, chunks * n_tok), bf16),
+            jax.ShapeDtypeStruct((chunks * n_tok, n_ex * block), bf16),
             weight_struct,
             weight_struct,
             weight_struct,
         ),
-        in_specs=[vmem] * 9,
-        out_specs=(vmem,) * 5,
+        in_specs=[vmem] * 6 + [hbm] * 3,
+        out_specs=(vmem,) * 2 + (hbm,) * 3,
         scratch_shapes=[
+            pltpu.VMEM((n_ex * block, chunks * n_tok), bf16),
+            *[pltpu.VMEM((width, cols), bf16) for _ in range(6)],
             pltpu.VMEM((2, n_dp, n_ex, block, LANES), bf16),
             pltpu.VMEM((2, n_dp - 1, n_ex, block, LANES), bf16),
             pltpu.VMEM((2, n_dp, n_ex, block, LANES), bf16),
@@ -573,7 +627,8 @@
             pltpu.VMEM((3, n_dp, group_rows, width), bf16),
             pltpu.VMEM((2, n_dp - 1, n_ex, block, LANES), bf16),
             pltpu.VMEM((2, n_dp, n_ex, block, LANES), bf16),
-            pltpu.VMEM((chunks, group_rows, n_ex * block), bf16),
+            pltpu.VMEM((n_ex * block, n_ex * block), bf16),
+            pltpu.VMEM((n_ex * block, n_ex * block), bf16),
             dma((2, n_dp)),
             dma((2, n_dp)),
             dma((2, n_dp, n_ex)),
@@ -586,6 +641,8 @@
             dma((2, n_dp)),
             dma((2, n_dp, n_ex)),
             dma((2, n_dp, n_ex)),
+            dma((3,)),
+            dma((3,)),
         ],
         compiler_params=pltpu.CompilerParams(
             collective_id=0, has_side_effects=True, vmem_limit_bytes=vmem_limit
@@ -597,7 +654,7 @@
         ),
     )(
         expert_ids.reshape(1, n_tok),
-        route_weight,
+        weight_row,
         jnp.asarray(key)[:, None],
         jnp.asarray(key)[None, :],
         tokens,
@@ -606,7 +663,6 @@
         w_up,
         w_down,
     )
-    hbm = pl.BlockSpec(memory_space=pl.ANY)
     return pl.pallas_call(
         finish_kernel,
         out_shape=(token_struct, token_struct, weight_struct, weight_struct, weight_struct),
@@ -614,7 +670,7 @@
         out_specs=(vmem,) * 2 + (hbm,) * 3,
         scratch_shapes=[pltpu.VMEM((3, width, cols), bf16), dma((3,)), dma((3,))],
         compiler_params=pltpu.CompilerParams(vmem_limit_bytes=vmem_limit),
-    )(route_weight, big, final, gate_grad, up_grad, down_grad)
+    )(weight_row, big_t, final, gate_grad, up_grad, down_grad)
 
 
 def solution(mesh):

time: 128 us -> 125 us (0.977)
  Pallas kernels: 126 us -> 124 us
  local copies, waits for them, and re-layouts: 1.4 us -> 0 us
    pallas_call x1, Pallas kernels: 120 us -> 119 us  [local_fused(): pl.pallas_call(functools.partial(fused_kernel, n_dp), out_shape=(jax.Shap...]
    unnamed x1 -> x0, local copies, waits for them, and re-layouts: 1.4 us -> none
where the time goes in v5:
time: 125 us
  Pallas kernels  124 us (99%)
    pallas_call x1, Pallas kernels, local_fused(): pl.pallas_call(functools.partial(fused_kernel, n_dp), out_shape=(jax.Shap...  119 us
    pallas_call x1, Pallas kernels, local_fused(): pl.pallas_call(finish_kernel, out_shape=(token_struct, token_struct, weig...  5.44 us

profile of v5, /device:TPU:0, one launch (start us, length us, event | category | flops | bytes accessed | tf_op | source)
XLA Modules:
  0.0 125.1 jit_solution(3763709758250942631)
XLA Ops:
  0.6 118.8 %shard_map.119 = (bf16[2,4,8,80,128]{4,3,2,1,0:T(8,128)(2,1)}, bf16[512,640]{1,0:T(8,128)(2,1)}, bf16[1024,512]{1,0:T(8,128)(2,1)}, bf16[1024,512]{1,0:T(8,128)(2,1)}, bf16[1024,512]{1,0:T(8,128)(2,1)}) custom-call(s32[1,128]{1,0:T(1,128)} %bitcast.4, f32[1,128]{1,0:T(1,128)} %bitcast.2, s32[640,1]{1,0:T(8,128)} %constant.3.row_key_ref, ...), custom_call_target="tpu_custom_call" | custom-call | flops 6039797760 | bytes 8388608 | tf_op jit(solution)/shard_map/pallas_call | solution.py:605
  119.5 5.4 %shard_map.120 = (bf16[128,2048]{1,0:T(8,128)(2,1)}, bf16[128,2048]{1,0:T(8,128)(2,1)}, bf16[1024,512]{1,0:T(8,128)(2,1)}, bf16[1024,512]{1,0:T(8,128)(2,1)}, bf16[1024,512]{1,0:T(8,128)(2,1)}) custom-call(f32[1,128]{1,0:T(1,128)} %bitcast.3, bf16[512,640]{1,0:T(8,128)(2,1)} %get-tuple-element.10.big_ref, ...), custom_call_target="tpu_custom_call" | custom-call | tf_op jit(solution)/shard_map/pallas_call | solution.py:666

commit v6 on v5

--- a/solution.py
+++ b/solution.py
@@ -414,11 +414,6 @@
     up_pre = total(1)
     share(0, (silu * up_pre).astype(jnp.bfloat16))
     own_partial[1] = up_pre * (sigmoid * (1.0 + gate_pre * (1.0 - sigmoid)))
-    relay_sum(2)
-    hidden_grad = total(2)
-    share(1, (hidden_grad * own_partial[1]).astype(jnp.bfloat16))
-    share(2, (hidden_grad * own_partial[0]).astype(jnp.bfloat16))
-
     def send_back(b, kd, value):
         value = value.astype(jnp.bfloat16)
         stack = jnp.concatenate(
@@ -488,20 +483,26 @@
         cp.start()
         stores.append(cp)
 
+    relay_sum(2)
+    output(0)
+    finish_send(0, 0)
     relay_hidden(0)
-    for kd in (1, 2, 0):
-        output(kd)
-    finish_send(0, 0)
-    relay_hidden(1)
-    relay_hidden(2)
+    output(1)
+    output(2)
+    hidden_grad = total(2)
+    share(1, (hidden_grad * own_partial[1]).astype(jnp.bfloat16))
+    share(2, (hidden_grad * own_partial[0]).astype(jnp.bfloat16))
     last_hidden(0)
     output(3)
     finish_send(0, 1)
     finish_send(0, 2)
-    for kd in (1, 2, 0):
-        input_grad(kd)
+    relay_hidden(1)
+    relay_hidden(2)
+    input_grad(0)
     finish_send(1, 0)
     finish_send(0, 3)
+    input_grad(1)
+    input_grad(2)
     last_hidden(1)
     last_hidden(2)
     input_grad(3)

time: 125 us -> 123 us (0.984)
  Pallas kernels: 124 us -> 122 us
    pallas_call x1, Pallas kernels: 119 us -> 116 us  [local_fused(): pl.pallas_call(functools.partial(fused_kernel, n_dp), out_shape=(jax.Shap...]
where the time goes in v6:
time: 123 us
  Pallas kernels  122 us (99%)
    pallas_call x1, Pallas kernels, local_fused(): pl.pallas_call(functools.partial(fused_kernel, n_dp), out_shape=(jax.Shap...  116 us
    pallas_call x1, Pallas kernels, local_fused(): pl.pallas_call(finish_kernel, out_shape=(token_struct, token_struct, weig...  5.44 us

profile of v6, /device:TPU:0, one launch (start us, length us, event | category | flops | bytes accessed | tf_op | source)
XLA Modules:
  0.0 122.5 jit_solution(2577251603931161474)
XLA Ops:
  0.6 116.3 %shard_map.119 = (bf16[2,4,8,80,128]{4,3,2,1,0:T(8,128)(2,1)}, bf16[512,640]{1,0:T(8,128)(2,1)}, bf16[1024,512]{1,0:T(8,128)(2,1)}, bf16[1024,512]{1,0:T(8,128)(2,1)}, bf16[1024,512]{1,0:T(8,128)(2,1)}) custom-call(s32[1,128]{1,0:T(1,128)} %bitcast.4, f32[1,128]{1,0:T(1,128)} %bitcast.2, s32[640,1]{1,0:T(8,128)} %constant.3.row_key_ref, ...), custom_call_target="tpu_custom_call" | custom-call | flops 6039797760 | bytes 8388608 | tf_op jit(solution)/shard_map/pallas_call | solution.py:606
  116.9 5.4 %shard_map.120 = (bf16[128,2048]{1,0:T(8,128)(2,1)}, bf16[128,2048]{1,0:T(8,128)(2,1)}, bf16[1024,512]{1,0:T(8,128)(2,1)}, bf16[1024,512]{1,0:T(8,128)(2,1)}, bf16[1024,512]{1,0:T(8,128)(2,1)}) custom-call(f32[1,128]{1,0:T(1,128)} %bitcast.3, bf16[512,640]{1,0:T(8,128)(2,1)} %get-tuple-element.10.big_ref, ...), custom_call_target="tpu_custom_call" | custom-call | tf_op jit(solution)/shard_map/pallas_call | solution.py:667
